TPU v7x, 256 devices: a whole 4x4x8 slice. The times are simulated.
256 devices in a mesh: patch: 32 (over y, z), visit: 8 (over x, core).
Axes of the slice: x: 4, y: 4, z: 8, core: 2. Of those that a mesh axis runs over, the one named last changes fastest.
Arguments:
- blocks: bfloat16 [8, 2048, 128, 128], P('visit', 'patch'), may hold values from -6 to 6
- send_list: int32 [8, 32, 2, 16], P('visit', 'patch'), may hold values from -1 to 63, as said below
- block_slot: int32 [8, 2048], P('visit', 'patch'), may hold values from 0 to 63, as said below
- block_offset: int32 [8, 2048, 2], P('visit', 'patch'), may hold values from -2 to 2
- block_frac: bfloat16 [8, 2048, 2], P('visit', 'patch'), may hold values from 0.049804688 to 0.94921875
- inv_var: bfloat16 [8, 2048], P('visit', 'patch'), may hold values from 0.29882812 to 3
- psf_kernel: float32 [8, 25, 25], P('visit'), may hold values from -0.24 to 0.24
Outputs:
- coadded: float32 [32768, 1024], P('patch', 'visit')
Inputs may be any that keep to these rules, and one draw needn't show every extreme that they name: `send_list`: each device's two lists hold distinct local blocks; device 0's list toward a lower patch and the last device's list toward a higher patch are all -1, every other list is full. `block_slot`: every slot of every patch receives exactly one block of every visit.
All inputs are finite; a program needn't handle non-finite values.
Results may differ from a plain program's by a relative error of at most 0.0066.
Values may be sent and summed in bfloat16 or wider, within the bound.
A program may use at most 64 MiB of HBM per device.

v0:
```python
import math

import jax
import jax.numpy as jnp
from jax import lax
from jax.sharding import PartitionSpec as P

SLOT_ROWS = 8
SLOT_COLS = 8
SLOTS = 64
KSIZE = 25


def extended(block, sides, width):
    for axis, dim in sides:
        count = lax.axis_size(axis)
        forward = [(i, i + 1) for i in range(count - 1)]
        backward = [(target, source) for source, target in forward]
        low = lax.ppermute(
            lax.slice_in_dim(block, block.shape[dim] - width, None, axis=dim), axis, forward
        )
        high = lax.ppermute(lax.slice_in_dim(block, 0, width, axis=dim), axis, backward)
        block = jnp.concatenate([low, block, high], axis=dim)
    return block


def lanczos_weight(tap_offset):
    inside = (jnp.abs(tap_offset) < 3.0) & (jnp.abs(tap_offset) > 0.001)
    safe_tap = jnp.where(inside, tap_offset, 1.5)
    value = (
        3.0
        * jnp.sin(math.pi * safe_tap)
        * jnp.sin(math.pi * safe_tap / 3.0)
        / (math.pi * math.pi * safe_tap * safe_tap)
    )
    return jnp.where(inside, value, 0.0)


def lanczos_matrix(shift, edge_len):
    positions = jnp.arange(edge_len).astype(jnp.float32)
    tap_offset = positions[None, None, :] - positions[None, :, None] - shift[:, None, None]
    return lanczos_weight(tap_offset).astype(jnp.bfloat16)


def warp_blocks(pixels, shift_info):
    edge_len = pixels.shape[-1]
    shift_info = shift_info.astype(jnp.float32)
    row_mat = lanczos_matrix(shift_info[:, 0] + shift_info[:, 2], edge_len)
    col_mat = lanczos_matrix(shift_info[:, 1] + shift_info[:, 3], edge_len)
    first = jnp.einsum("nim,nmk->nik", row_mat, pixels, preferred_element_type=jnp.float32).astype(
        jnp.bfloat16
    )
    return jnp.einsum("nik,njk->nij", first, col_mat, preferred_element_type=jnp.float32).astype(
        jnp.bfloat16
    )


def on_device(blocks, send_list, block_slot, block_offset, block_frac, inv_var, psf_kernel):
    pixels = blocks[0]
    edge_len = pixels.shape[-1]
    block_count = pixels.shape[0]
    block_lists = send_list[0, 0]
    side_count = block_lists.shape[1]
    is_live = block_lists >= 0
    picked = jnp.maximum(block_lists, 0)
    local_ids = jnp.arange(block_count)
    leaving = jnp.any((block_lists[..., None] == local_ids) & is_live[..., None], axis=(0, 1))
    slot_onehot = block_slot[0][:, None] == jnp.arange(SLOTS)[None, :]
    slot_weight = jnp.where(slot_onehot, inv_var[0][:, None], 0)
    local_w = jnp.where(leaving[:, None], 0, slot_weight)
    meta_info = jnp.concatenate([block_offset[0].astype(jnp.bfloat16), block_frac[0]], axis=1)
    weight_send = jnp.where(is_live[..., None], slot_weight[picked], 0)
    meta_send = jnp.where(is_live[..., None], meta_info[picked], 0.25)
    filler = jnp.zeros((2, side_count, edge_len - 4 - SLOTS), jnp.bfloat16)
    info_row = jnp.concatenate([meta_send, weight_send, filler], axis=2)[:, :, None, :]
    leaving_pixels = pixels[picked]
    payload = jnp.where(is_live[..., None, None], leaving_pixels, 0)
    packed = jnp.concatenate([payload, info_row], axis=2).reshape(
        2 * side_count, edge_len + 1, edge_len
    )
    beside_all = extended(packed, (("patch", 0),), side_count)
    incoming = jnp.concatenate([beside_all[:side_count], beside_all[3 * side_count :]], axis=0)
    in_pixels = incoming[:, :edge_len]
    in_info = incoming[:, edge_len]
    in_w = in_info[:, 4 : 4 + SLOTS]
    local_warped = warp_blocks(pixels, meta_info)
    in_warped = warp_blocks(in_pixels, in_info[:, :4])
    flat_w = jnp.concatenate([local_w, in_w], axis=0)
    flat_x = jnp.concatenate([local_warped, in_warped], axis=0).reshape(
        (flat_w.shape[0], edge_len * edge_len)
    )
    slot_sum = jnp.einsum("rs,rp->sp", flat_w, flat_x, preferred_element_type=jnp.float32)
    visit_image = (
        slot_sum.reshape(SLOT_ROWS, SLOT_COLS, edge_len, edge_len)
        .transpose(0, 2, 1, 3)
        .reshape(SLOT_ROWS * edge_len, SLOT_COLS * edge_len)
        .astype(jnp.bfloat16)
    )
    slot_denom = jnp.sum(flat_w.astype(jnp.float32), axis=0).reshape(SLOT_ROWS, SLOT_COLS)
    denom_cols = jnp.repeat(slot_denom, edge_len, axis=1)
    half_reach = KSIZE // 2
    padded = extended(visit_image, (("patch", 0),), half_reach)
    col_padded = jnp.pad(padded, ((0, 0), (half_reach, half_reach)))
    windows = jnp.stack(
        [
            col_padded[
                :, column_tile * edge_len : column_tile * edge_len + edge_len + 2 * half_reach
            ]
            for column_tile in range(SLOT_COLS)
        ],
        axis=1,
    )
    kernel = psf_kernel[0].astype(jnp.bfloat16)
    tap_lag = jnp.arange(edge_len + 2 * half_reach)[:, None] - jnp.arange(edge_len)[None, :]
    in_band = (tap_lag >= 0) & (tap_lag < KSIZE)
    toeplitz = jnp.where(in_band[None], kernel[:, jnp.clip(tap_lag, 0, KSIZE - 1)], 0)
    row_count = visit_image.shape[0]

    def add_row(kernel_row, running):
        row_band = lax.dynamic_slice_in_dim(windows, kernel_row, row_count, 0)
        row_taps = lax.dynamic_index_in_dim(toeplitz, kernel_row, 0, keepdims=False)
        return running + jnp.einsum(
            "rtk,kc->rtc", row_band, row_taps, preferred_element_type=jnp.float32
        )

    running = lax.fori_loop(
        0, KSIZE, add_row, jnp.zeros((row_count, SLOT_COLS, edge_len), jnp.float32)
    )
    blurred = running.reshape(row_count, SLOT_COLS * edge_len)
    numer_all, denom_all = lax.psum((blurred, denom_cols), "visit")
    share_cols = numer_all.shape[1] // lax.axis_size("visit")
    first_col = lax.axis_index("visit") * share_cols
    numer_share = lax.dynamic_slice_in_dim(numer_all, first_col, share_cols, 1)
    denom_share = lax.dynamic_slice_in_dim(denom_all, first_col, share_cols, 1)
    coadded = numer_share / jnp.repeat(denom_share, edge_len, axis=0)
    return coadded


def solution(mesh):
    in_specs = (
        P("visit", "patch", None, None),
        P("visit", "patch", None, None),
        P("visit", "patch"),
        P("visit", "patch", None),
        P("visit", "patch", None),
        P("visit", "patch"),
        P("visit", None, None),
    )
    out_specs = P("patch", "visit")
    return jax.shard_map(
        on_device, mesh=mesh, in_specs=in_specs, out_specs=out_specs, check_vma=False
    )
```

profile of v0, /device:TPU:24, one launch (start us, length us, event | category | flops | bytes accessed | tf_op | source)
XLA Modules:
  0.0 525.0 jit_solution(15611467892967527578)
XLA Ops:
  25.6 34.3 %fusion.189 = bf16[64,128,128]{2,1,0:T(8,128)(2,1)S(1)} fusion(f32[64]{0:T(128)S(1)} %get-tuple-element.114, f32[128,128]{1,0:T(8,128)S(1)} %broadcast_subtract_fusion, bf16[1,64,128,128]{3,2,1,0:T(8,128)(2,1)S(1)} %copy-done), kind=kOutput, calls=%fused_computation.80.clone.clone.clone.2 | convolution fusion | flops 285212672 | bytes 4260096 | tf_op jit(solution)/shard_map/nim,nmk->nik/dot_general | solution.py:50
  59.9 33.1 %fusion.86 = bf16[64,128,128]{2,1,0:T(8,128)(2,1)} fusion(f32[64]{0:T(128)S(1)} %get-tuple-element.115, f32[128,128]{1,0:T(8,128)S(1)} %broadcast_subtract_fusion, bf16[64,128,128]{2,1,0:T(8,128)(2,1)S(1)} %fusion.189), kind=kOutput, calls=%fused_computation.93 | convolution fusion | flops 285212672 | bytes 4260096 | tf_op jit(solution)/shard_map/nik,njk->nij/dot_general | solution.py:53
  93.1 68.0 %gather_fusion.3 = bf16[19456,25]{1,0:T(8,128)(2,1)} fusion(bf16[25,25]{0,1:T(8,128)(2,1)S(1)} %bitcast.125, s32[19456]{0:T(1024)S(1)} %fusion.131), kind=kCustom, calls=%fused_computation.3 | custom fusion | bytes 2023424 | tf_op jit(solution)/shard_map/gather | solution.py:116
  169.0 34.9 %convolution_convert_fusion = bf16[32,128,128]{2,1,0:T(8,128)(2,1)} fusion(bf16[32,129,128]{2,1,0:T(8,128)(2,1)} %copy-done.3, f32[32]{0:T(128)S(1)} %get-tuple-element.101, f32[32]{0:T(128)S(1)} %get-tuple-element.100, f32[128,128]{1,0:T(8,128)S(1)} %broadcast_subtract_fusion), kind=kOutput, calls=%fused_computation.94 | convolution fusion | flops 285212672 | bytes 2229248 | tf_op jit(solution)/shard_map/nik,njk->nij/dot_general | solution.py:53
  239.0 194.6 %while.14 = (s32[]{:T(128)}, f32[1024,8,128]{2,0,1:T(8,128)}, bf16[1048,8,152]{0,2,1:T(8,128)(2,1)}, bf16[25,152,128]{2,1,0:T(8,128)(2,1)}, s32[]{:T(128)}, /*index=5*/s32[]{:T(128)}) while((s32[]{:T(128)}, f32[1024,8,128]{2,0,1:T(8,128)}, bf16[1048,8,152]{0,2,1:T(8,128)(2,1)}, bf16[25,152,128]{2,1,0:T(8,128)(2,1)}, s32[]{:T(128)}, ...), condition=%wide.region_2.3_spmd.clone, body=%wide.region_1.2_spmd.clone.sunk | while | flops 320864256 | bytes 10918991 | solution.py:126
  239.0 6.6 %select_add_fusion.2 = f32[1024,8,128]{2,0,1:T(8,128)} fusion(f32[1024,8,128]{2,0,1:T(8,128)} %get-tuple-element.152, bf16[1048,8,152]{0,2,1:T(8,128)(2,1)} %get-tuple-element.159, s32[]{:T(128)} %get-tuple-element.151, pred[]{:T(512)S(6)} %compare.4, bf16[25,152,128]{2,1,0:T(8,128)(2,1)} %get-tuple-element.160), kind=kOutput, calls=%fused_computation.4.clone.1 | convolution fusion | flops 320864256 | bytes 10918913 | tf_op jit(solution)/shard_map/while/body/eval_jaxpr/rtk,kc->rtc/dot_general | solution.py:122
  245.6 7.8 %select_add_fusion.2 = f32[1024,8,128]{2,0,1:T(8,128)} fusion(f32[1024,8,128]{2,0,1:T(8,128)} %get-tuple-element.152, bf16[1048,8,152]{0,2,1:T(8,128)(2,1)} %get-tuple-element.159, s32[]{:T(128)} %get-tuple-element.151, pred[]{:T(512)S(6)} %compare.4, bf16[25,152,128]{2,1,0:T(8,128)(2,1)} %get-tuple-element.160), kind=kOutput, calls=%fused_computation.4.clone.1 | convolution fusion | flops 320864256 | bytes 10918913 | tf_op jit(solution)/shard_map/while/body/eval_jaxpr/rtk,kc->rtc/dot_general | solution.py:122
  253.4 7.8 %select_add_fusion.2 = f32[1024,8,128]{2,0,1:T(8,128)} fusion(f32[1024,8,128]{2,0,1:T(8,128)} %get-tuple-element.152, bf16[1048,8,152]{0,2,1:T(8,128)(2,1)} %get-tuple-element.159, s32[]{:T(128)} %get-tuple-element.151, pred[]{:T(512)S(6)} %compare.4, bf16[25,152,128]{2,1,0:T(8,128)(2,1)} %get-tuple-element.160), kind=kOutput, calls=%fused_computation.4.clone.1 | convolution fusion | flops 320864256 | bytes 10918913 | tf_op jit(solution)/shard_map/while/body/eval_jaxpr/rtk,kc->rtc/dot_general | solution.py:122
  261.3 7.8 %select_add_fusion.2 = f32[1024,8,128]{2,0,1:T(8,128)} fusion(f32[1024,8,128]{2,0,1:T(8,128)} %get-tuple-element.152, bf16[1048,8,152]{0,2,1:T(8,128)(2,1)} %get-tuple-element.159, s32[]{:T(128)} %get-tuple-element.151, pred[]{:T(512)S(6)} %compare.4, bf16[25,152,128]{2,1,0:T(8,128)(2,1)} %get-tuple-element.160), kind=kOutput, calls=%fused_computation.4.clone.1 | convolution fusion | flops 320864256 | bytes 10918913 | tf_op jit(solution)/shard_map/while/body/eval_jaxpr/rtk,kc->rtc/dot_general | solution.py:122
  269.1 7.8 %select_add_fusion.2 = f32[1024,8,128]{2,0,1:T(8,128)} fusion(f32[1024,8,128]{2,0,1:T(8,128)} %get-tuple-element.152, bf16[1048,8,152]{0,2,1:T(8,128)(2,1)} %get-tuple-element.159, s32[]{:T(128)} %get-tuple-element.151, pred[]{:T(512)S(6)} %compare.4, bf16[25,152,128]{2,1,0:T(8,128)(2,1)} %get-tuple-element.160), kind=kOutput, calls=%fused_computation.4.clone.1 | convolution fusion | flops 320864256 | bytes 10918913 | tf_op jit(solution)/shard_map/while/body/eval_jaxpr/rtk,kc->rtc/dot_general | solution.py:122
  277.0 7.8 %select_add_fusion.2 = f32[1024,8,128]{2,0,1:T(8,128)} fusion(f32[1024,8,128]{2,0,1:T(8,128)} %get-tuple-element.152, bf16[1048,8,152]{0,2,1:T(8,128)(2,1)} %get-tuple-element.159, s32[]{:T(128)} %get-tuple-element.151, pred[]{:T(512)S(6)} %compare.4, bf16[25,152,128]{2,1,0:T(8,128)(2,1)} %get-tuple-element.160), kind=kOutput, calls=%fused_computation.4.clone.1 | convolution fusion | flops 320864256 | bytes 10918913 | tf_op jit(solution)/shard_map/while/body/eval_jaxpr/rtk,kc->rtc/dot_general | solution.py:122
  284.8 7.8 %select_add_fusion.2 = f32[1024,8,128]{2,0,1:T(8,128)} fusion(f32[1024,8,128]{2,0,1:T(8,128)} %get-tuple-element.152, bf16[1048,8,152]{0,2,1:T(8,128)(2,1)} %get-tuple-element.159, s32[]{:T(128)} %get-tuple-element.151, pred[]{:T(512)S(6)} %compare.4, bf16[25,152,128]{2,1,0:T(8,128)(2,1)} %get-tuple-element.160), kind=kOutput, calls=%fused_computation.4.clone.1 | convolution fusion | flops 320864256 | bytes 10918913 | tf_op jit(solution)/shard_map/while/body/eval_jaxpr/rtk,kc->rtc/dot_general | solution.py:122
  292.6 7.8 %select_add_fusion.2 = f32[1024,8,128]{2,0,1:T(8,128)} fusion(f32[1024,8,128]{2,0,1:T(8,128)} %get-tuple-element.152, bf16[1048,8,152]{0,2,1:T(8,128)(2,1)} %get-tuple-element.159, s32[]{:T(128)} %get-tuple-element.151, pred[]{:T(512)S(6)} %compare.4, bf16[25,152,128]{2,1,0:T(8,128)(2,1)} %get-tuple-element.160), kind=kOutput, calls=%fused_computation.4.clone.1 | convolution fusion | flops 320864256 | bytes 10918913 | tf_op jit(solution)/shard_map/while/body/eval_jaxpr/rtk,kc->rtc/dot_general | solution.py:122
  300.5 7.8 %select_add_fusion.2 = f32[1024,8,128]{2,0,1:T(8,128)} fusion(f32[1024,8,128]{2,0,1:T(8,128)} %get-tuple-element.152, bf16[1048,8,152]{0,2,1:T(8,128)(2,1)} %get-tuple-element.159, s32[]{:T(128)} %get-tuple-element.151, pred[]{:T(512)S(6)} %compare.4, bf16[25,152,128]{2,1,0:T(8,128)(2,1)} %get-tuple-element.160), kind=kOutput, calls=%fused_computation.4.clone.1 | convolution fusion | flops 320864256 | bytes 10918913 | tf_op jit(solution)/shard_map/while/body/eval_jaxpr/rtk,kc->rtc/dot_general | solution.py:122
  308.3 7.8 %select_add_fusion.2 = f32[1024,8,128]{2,0,1:T(8,128)} fusion(f32[1024,8,128]{2,0,1:T(8,128)} %get-tuple-element.152, bf16[1048,8,152]{0,2,1:T(8,128)(2,1)} %get-tuple-element.159, s32[]{:T(128)} %get-tuple-element.151, pred[]{:T(512)S(6)} %compare.4, bf16[25,152,128]{2,1,0:T(8,128)(2,1)} %get-tuple-element.160), kind=kOutput, calls=%fused_computation.4.clone.1 | convolution fusion | flops 320864256 | bytes 10918913 | tf_op jit(solution)/shard_map/while/body/eval_jaxpr/rtk,kc->rtc/dot_general | solution.py:122
  316.1 7.8 %select_add_fusion.2 = f32[1024,8,128]{2,0,1:T(8,128)} fusion(f32[1024,8,128]{2,0,1:T(8,128)} %get-tuple-element.152, bf16[1048,8,152]{0,2,1:T(8,128)(2,1)} %get-tuple-element.159, s32[]{:T(128)} %get-tuple-element.151, pred[]{:T(512)S(6)} %compare.4, bf16[25,152,128]{2,1,0:T(8,128)(2,1)} %get-tuple-element.160), kind=kOutput, calls=%fused_computation.4.clone.1 | convolution fusion | flops 320864256 | bytes 10918913 | tf_op jit(solution)/shard_map/while/body/eval_jaxpr/rtk,kc->rtc/dot_general | solution.py:122
  324.0 7.8 %select_add_fusion.2 = f32[1024,8,128]{2,0,1:T(8,128)} fusion(f32[1024,8,128]{2,0,1:T(8,128)} %get-tuple-element.152, bf16[1048,8,152]{0,2,1:T(8,128)(2,1)} %get-tuple-element.159, s32[]{:T(128)} %get-tuple-element.151, pred[]{:T(512)S(6)} %compare.4, bf16[25,152,128]{2,1,0:T(8,128)(2,1)} %get-tuple-element.160), kind=kOutput, calls=%fused_computation.4.clone.1 | convolution fusion | flops 320864256 | bytes 10918913 | tf_op jit(solution)/shard_map/while/body/eval_jaxpr/rtk,kc->rtc/dot_general | solution.py:122
  331.8 7.8 %select_add_fusion.2 = f32[1024,8,128]{2,0,1:T(8,128)} fusion(f32[1024,8,128]{2,0,1:T(8,128)} %get-tuple-element.152, bf16[1048,8,152]{0,2,1:T(8,128)(2,1)} %get-tuple-element.159, s32[]{:T(128)} %get-tuple-element.151, pred[]{:T(512)S(6)} %compare.4, bf16[25,152,128]{2,1,0:T(8,128)(2,1)} %get-tuple-element.160), kind=kOutput, calls=%fused_computation.4.clone.1 | convolution fusion | flops 320864256 | bytes 10918913 | tf_op jit(solution)/shard_map/while/body/eval_jaxpr/rtk,kc->rtc/dot_general | solution.py:122
  339.6 7.8 %select_add_fusion.2 = f32[1024,8,128]{2,0,1:T(8,128)} fusion(f32[1024,8,128]{2,0,1:T(8,128)} %get-tuple-element.152, bf16[1048,8,152]{0,2,1:T(8,128)(2,1)} %get-tuple-element.159, s32[]{:T(128)} %get-tuple-element.151, pred[]{:T(512)S(6)} %compare.4, bf16[25,152,128]{2,1,0:T(8,128)(2,1)} %get-tuple-element.160), kind=kOutput, calls=%fused_computation.4.clone.1 | convolution fusion | flops 320864256 | bytes 10918913 | tf_op jit(solution)/shard_map/while/body/eval_jaxpr/rtk,kc->rtc/dot_general | solution.py:122
  347.5 7.8 %select_add_fusion.2 = f32[1024,8,128]{2,0,1:T(8,128)} fusion(f32[1024,8,128]{2,0,1:T(8,128)} %get-tuple-element.152, bf16[1048,8,152]{0,2,1:T(8,128)(2,1)} %get-tuple-element.159, s32[]{:T(128)} %get-tuple-element.151, pred[]{:T(512)S(6)} %compare.4, bf16[25,152,128]{2,1,0:T(8,128)(2,1)} %get-tuple-element.160), kind=kOutput, calls=%fused_computation.4.clone.1 | convolution fusion | flops 320864256 | bytes 10918913 | tf_op jit(solution)/shard_map/while/body/eval_jaxpr/rtk,kc->rtc/dot_general | solution.py:122
  355.3 7.8 %select_add_fusion.2 = f32[1024,8,128]{2,0,1:T(8,128)} fusion(f32[1024,8,128]{2,0,1:T(8,128)} %get-tuple-element.152, bf16[1048,8,152]{0,2,1:T(8,128)(2,1)} %get-tuple-element.159, s32[]{:T(128)} %get-tuple-element.151, pred[]{:T(512)S(6)} %compare.4, bf16[25,152,128]{2,1,0:T(8,128)(2,1)} %get-tuple-element.160), kind=kOutput, calls=%fused_computation.4.clone.1 | convolution fusion | flops 320864256 | bytes 10918913 | tf_op jit(solution)/shard_map/while/body/eval_jaxpr/rtk,kc->rtc/dot_general | solution.py:122
  363.1 7.8 %select_add_fusion.2 = f32[1024,8,128]{2,0,1:T(8,128)} fusion(f32[1024,8,128]{2,0,1:T(8,128)} %get-tuple-element.152, bf16[1048,8,152]{0,2,1:T(8,128)(2,1)} %get-tuple-element.159, s32[]{:T(128)} %get-tuple-element.151, pred[]{:T(512)S(6)} %compare.4, bf16[25,152,128]{2,1,0:T(8,128)(2,1)} %get-tuple-element.160), kind=kOutput, calls=%fused_computation.4.clone.1 | convolution fusion | flops 320864256 | bytes 10918913 | tf_op jit(solution)/shard_map/while/body/eval_jaxpr/rtk,kc->rtc/dot_general | solution.py:122
  371.0 7.8 %select_add_fusion.2 = f32[1024,8,128]{2,0,1:T(8,128)} fusion(f32[1024,8,128]{2,0,1:T(8,128)} %get-tuple-element.152, bf16[1048,8,152]{0,2,1:T(8,128)(2,1)} %get-tuple-element.159, s32[]{:T(128)} %get-tuple-element.151, pred[]{:T(512)S(6)} %compare.4, bf16[25,152,128]{2,1,0:T(8,128)(2,1)} %get-tuple-element.160), kind=kOutput, calls=%fused_computation.4.clone.1 | convolution fusion | flops 320864256 | bytes 10918913 | tf_op jit(solution)/shard_map/while/body/eval_jaxpr/rtk,kc->rtc/dot_general | solution.py:122
  378.8 7.8 %select_add_fusion.2 = f32[1024,8,128]{2,0,1:T(8,128)} fusion(f32[1024,8,128]{2,0,1:T(8,128)} %get-tuple-element.152, bf16[1048,8,152]{0,2,1:T(8,128)(2,1)} %get-tuple-element.159, s32[]{:T(128)} %get-tuple-element.151, pred[]{:T(512)S(6)} %compare.4, bf16[25,152,128]{2,1,0:T(8,128)(2,1)} %get-tuple-element.160), kind=kOutput, calls=%fused_computation.4.clone.1 | convolution fusion | flops 320864256 | bytes 10918913 | tf_op jit(solution)/shard_map/while/body/eval_jaxpr/rtk,kc->rtc/dot_general | solution.py:122
  386.7 7.8 %select_add_fusion.2 = f32[1024,8,128]{2,0,1:T(8,128)} fusion(f32[1024,8,128]{2,0,1:T(8,128)} %get-tuple-element.152, bf16[1048,8,152]{0,2,1:T(8,128)(2,1)} %get-tuple-element.159, s32[]{:T(128)} %get-tuple-element.151, pred[]{:T(512)S(6)} %compare.4, bf16[25,152,128]{2,1,0:T(8,128)(2,1)} %get-tuple-element.160), kind=kOutput, calls=%fused_computation.4.clone.1 | convolution fusion | flops 320864256 | bytes 10918913 | tf_op jit(solution)/shard_map/while/body/eval_jaxpr/rtk,kc->rtc/dot_general | solution.py:122
  394.5 7.8 %select_add_fusion.2 = f32[1024,8,128]{2,0,1:T(8,128)} fusion(f32[1024,8,128]{2,0,1:T(8,128)} %get-tuple-element.152, bf16[1048,8,152]{0,2,1:T(8,128)(2,1)} %get-tuple-element.159, s32[]{:T(128)} %get-tuple-element.151, pred[]{:T(512)S(6)} %compare.4, bf16[25,152,128]{2,1,0:T(8,128)(2,1)} %get-tuple-element.160), kind=kOutput, calls=%fused_computation.4.clone.1 | convolution fusion | flops 320864256 | bytes 10918913 | tf_op jit(solution)/shard_map/while/body/eval_jaxpr/rtk,kc->rtc/dot_general | solution.py:122
  402.3 7.8 %select_add_fusion.2 = f32[1024,8,128]{2,0,1:T(8,128)} fusion(f32[1024,8,128]{2,0,1:T(8,128)} %get-tuple-element.152, bf16[1048,8,152]{0,2,1:T(8,128)(2,1)} %get-tuple-element.159, s32[]{:T(128)} %get-tuple-element.151, pred[]{:T(512)S(6)} %compare.4, bf16[25,152,128]{2,1,0:T(8,128)(2,1)} %get-tuple-element.160), kind=kOutput, calls=%fused_computation.4.clone.1 | convolution fusion | flops 320864256 | bytes 10918913 | tf_op jit(solution)/shard_map/while/body/eval_jaxpr/rtk,kc->rtc/dot_general | solution.py:122
  410.2 7.8 %select_add_fusion.2 = f32[1024,8,128]{2,0,1:T(8,128)} fusion(f32[1024,8,128]{2,0,1:T(8,128)} %get-tuple-element.152, bf16[1048,8,152]{0,2,1:T(8,128)(2,1)} %get-tuple-element.159, s32[]{:T(128)} %get-tuple-element.151, pred[]{:T(512)S(6)} %compare.4, bf16[25,152,128]{2,1,0:T(8,128)(2,1)} %get-tuple-element.160), kind=kOutput, calls=%fused_computation.4.clone.1 | convolution fusion | flops 320864256 | bytes 10918913 | tf_op jit(solution)/shard_map/while/body/eval_jaxpr/rtk,kc->rtc/dot_general | solution.py:122
  418.0 7.8 %select_add_fusion.2 = f32[1024,8,128]{2,0,1:T(8,128)} fusion(f32[1024,8,128]{2,0,1:T(8,128)} %get-tuple-element.152, bf16[1048,8,152]{0,2,1:T(8,128)(2,1)} %get-tuple-element.159, s32[]{:T(128)} %get-tuple-element.151, pred[]{:T(512)S(6)} %compare.4, bf16[25,152,128]{2,1,0:T(8,128)(2,1)} %get-tuple-element.160), kind=kOutput, calls=%fused_computation.4.clone.1 | convolution fusion | flops 320864256 | bytes 10918913 | tf_op jit(solution)/shard_map/while/body/eval_jaxpr/rtk,kc->rtc/dot_general | solution.py:122
  425.8 7.8 %select_add_fusion.2 = f32[1024,8,128]{2,0,1:T(8,128)} fusion(f32[1024,8,128]{2,0,1:T(8,128)} %get-tuple-element.152, bf16[1048,8,152]{0,2,1:T(8,128)(2,1)} %get-tuple-element.159, s32[]{:T(128)} %get-tuple-element.151, pred[]{:T(512)S(6)} %compare.4, bf16[25,152,128]{2,1,0:T(8,128)(2,1)} %get-tuple-element.160), kind=kOutput, calls=%fused_computation.4.clone.1 | convolution fusion | flops 320864256 | bytes 10918913 | tf_op jit(solution)/shard_map/while/body/eval_jaxpr/rtk,kc->rtc/dot_general | solution.py:122
  438.7 24.3 %psum.15 = f32[8,1024]{1,0:T(8,128)S(1)} all-reduce(f32[8,1024]{1,0:T(8,128)S(1)} %broadcast_bitcast_fusion), channel_id=1, replica_groups=mesh['patch'=32,'visit'=8] {'visit'}, use_global_device_ids=true, to_apply=%region_5.6 | all-reduce | flops 8192 | bytes 65536 | tf_op jit(solution)/shard_map/psum | solution.py:130
  463.0 53.3 %all-reduce.3.cloned.1.call-done = f32[1024,1024]{1,0:T(8,128)} async-done(((f32[1024,1024]{1,0:T(8,128)}), f32[1024,1024]{1,0:T(8,128)}) %all-reduce.3.cloned.1.call-update) | async-done | bytes 4194320 | tf_op jit(solution)/shard_map/psum | solution.py:130
  (83 shorter events, 68.8 us)
Async XLA Ops:
  6.5 6.3 %copy-start = (bf16[1,64,128,128]{3,2,1,0:T(8,128)(2,1)S(1)}, bf16[1,64,128,128]{3,2,1,0:T(8,128)(2,1)}, u32[]{:S(2)}) copy-start(bf16[1,64,128,128]{3,2,1,0:T(8,128)(2,1)} %param.9) | copy-start | bytes 6291460
  6.5 509.8 %all-reduce.3.cloned.1.call-start = ((), (), s32[]{:S(2)}) async-start(), calls=%async_computation | async-start | bytes 8388608 | tf_op jit(solution)/shard_map/psum | solution.py:130
  14.7 150.8 %collective-permute-start = (bf16[16,129,128]{2,0,1:T(8,128)(2,1)}, bf16[16,129,128]{2,0,1:T(8,128)(2,1)}, u32[]{:S(2)}, u32[]{:S(2)}) collective-permute-start(bf16[16,129,128]{2,0,1:T(8,128)(2,1)} %copy.63), channel_id=1, source_target_pairs={{0,8},{8,16},{16,24},{24,32},{32,40},{40,48},{48,56},{56,64},{64,7... | collective-permute-start | bytes 1585160 | tf_op jit(solution)/shard_map/ppermute | solution.py:19
  19.4 147.2 %collective-permute-start.1 = (bf16[16,129,128]{2,0,1:T(8,128)(2,1)}, bf16[16,129,128]{2,0,1:T(8,128)(2,1)}, u32[]{:S(2)}, u32[]{:S(2)}) collective-permute-start(bf16[16,129,128]{2,0,1:T(8,128)(2,1)} %copy.64), channel_id=1, source_target_pairs={{8,0},{16,8},{24,16},{32,24},{40,32},{48,40},{56,48},{64,56},{72,6... | collective-permute-start | bytes 1585160 | tf_op jit(solution)/shard_map/ppermute | solution.py:22
  59.8 33.2 %copy-start.4 = (f32[1,25,25]{2,0,1:T(1,128)S(1)}, f32[1,25,25]{2,0,1:T(1,128)}, u32[]{:S(2)}) copy-start(f32[1,25,25]{2,0,1:T(1,128)} %param.15) | copy-start | bytes 7504
  167.9 1.0 copy-start.3
  216.3 12.0 %collective-permute-start.2 = (bf16[12,1024]{0,1:T(8,128)(2,1)}, bf16[12,1024]{0,1:T(8,128)(2,1)S(1)}, u32[]{:S(2)}, u32[]{:S(2)}) collective-permute-start(bf16[12,1024]{0,1:T(8,128)(2,1)} %get-tuple-element.111), channel_id=1, source_target_pairs={{0,8},{8,16},{16,24},{24,32},{32,40},{40,48},{48,56},{56,64},{64,7... | collective-permute-start | bytes 73736 | tf_op jit(solution)/shard_map/ppermute | solution.py:19
  218.2 11.3 %collective-permute-start.3 = (bf16[12,1024]{0,1:T(8,128)(2,1)}, bf16[12,1024]{0,1:T(8,128)(2,1)}, u32[]{:S(2)}, u32[]{:S(2)}) collective-permute-start(bf16[12,1024]{0,1:T(8,128)(2,1)} %get-tuple-element.110), channel_id=1, source_target_pairs={{8,0},{16,8},{24,16},{32,24},{40,32},{48,40},{56,48},{64,56},{72,6... | collective-permute-start | bytes 73736 | tf_op jit(solution)/shard_map/ppermute | solution.py:22
  234.9 1.8 copy-start.2
  237.4 1.6 copy-start.1
Sparse Core Ops, SparseCore 0:
  438.5 77.7 all-reduce.2
where the time goes:
time: 526 us; the launch traced here: 525 us
  matrix products  299 us (57%)
  local copies, waits for them, and re-layouts  102 us (19%)
  waiting for transfers between devices  57.4 us (11%)
  blocking collectives  24.3 us (5%)
  starting transfers between devices  17.8 us (3%)
  between operations  13.7 us (3%)
  other arithmetic  10.5 us (2%)
    dot_general x25, matrix products, add_row(): jnp.einsum('rtk,kc->rtc', row_band, row_taps, preferred_element_type=jnp....  195 us
    gather x2, local copies, waits for them, and re-layouts, on_device(): kernel[:, jnp.clip(tap_lag, 0, KSIZE - 1)]  72.3 us
    dot_general x2, matrix products, warp_blocks(): jnp.einsum('nik,njk->nij', first, col_mat, preferred_element_type=jnp.flo...  68 us
    psum x1, waiting for transfers between devices, on_device(): numer_all, denom_all = lax.psum((blurred, denom_cols), 'visit')  53.3 us
    dot_general x1, matrix products, warp_blocks(): jnp.einsum('nim,nmk->nik', row_mat, pixels, preferred_element_type=jnp.fl...  34.3 us
    psum x1, blocking collectives, on_device(): numer_all, denom_all = lax.psum((blurred, denom_cols), 'visit')  24.3 us
    ppermute x2, starting transfers between devices, extended(): lax.ppermute(lax.slice_in_dim(block, 0, width, axis=dim), axis, backward)  12.1 us
  transfers between devices with their start and end apart: 5, of which 3 were waited for; matrix products, arithmetic and copies ran while one was open for 27% of the time, Pallas kernels for 0%

commit v1 on v0

v1 whole, which is shorter than its diff:
```python
import math

import jax
import jax.numpy as jnp
from jax import lax
from jax.experimental import pallas as pl
from jax.experimental.pallas import tpu as pltpu
from jax.sharding import PartitionSpec as P

EDGE = 128
BLOCKS = 64
CAP = 16
KSIZE = 25
REACH = 12
GROUP = 8
SLOT_COLS = 8
SLOT_ROWS = 8
ROWS = SLOT_ROWS * EDGE
COLS = SLOT_COLS * EDGE
HALO = 16
EXT_ROWS = ROWS + 2 * HALO
SEGS = 16
SEG_ROWS = ROWS // SEGS
PAIRS = SEG_ROWS // 2
STEPS = KSIZE // 2 + 1
EXT_PAIRS = PAIRS + STEPS - 1
OUT_WIN = EDGE - 2 * REACH
WINDOWS = -(-COLS // OUT_WIN)
F32 = jnp.float32
BF16 = jnp.bfloat16


def lanczos_weight(tap_offset):
    inside = jnp.abs(tap_offset) < 3.0
    safe_tap = jnp.where(inside, tap_offset, 1.5)
    value = (
        3.0
        * jnp.sin(math.pi * safe_tap)
        * jnp.sin(math.pi * safe_tap / 3.0)
        / (math.pi * math.pi * safe_tap * safe_tap)
    )
    return jnp.where(inside, value, 0.0)


def column_of(row):
    count = row.shape[1]
    down = lax.broadcasted_iota(jnp.int32, (count, count), 0)
    across = lax.broadcasted_iota(jnp.int32, (count, count), 1)
    spread = jnp.where(down == across, jnp.broadcast_to(row, (count, count)), 0.0)
    return jnp.sum(spread, axis=1, keepdims=True)


def warp_kernel(
    list_ref,
    slot_ref,
    list_vec,
    slot_vec,
    offset_ref,
    frac_ref,
    weight_ref,
    blocks_ref,
    own_ref,
    index_ref,
    slot_weight_ref,
    row_taps,
    col_taps,
    weights,
    place,
):
    step = pl.program_id(0)
    patch = lax.axis_index("patch")
    last = lax.axis_size("patch") - 1

    @pl.when(step == 0)
    def prepare():
        shift = offset_ref[...].astype(F32) + frac_ref[...].astype(F32)
        lane = lax.broadcasted_iota(jnp.int32, (BLOCKS, EDGE), 1)
        signed = jnp.where(lane < EDGE // 2, lane, lane - EDGE).astype(F32)
        row_taps[...] = lanczos_weight(signed - shift[:, 0:1]).astype(BF16).astype(F32)
        col_taps[...] = lanczos_weight(-signed - shift[:, 1:2]).astype(BF16).astype(F32)
        weight = column_of(weight_ref[...].astype(F32))
        weights[...] = jnp.broadcast_to(weight, (BLOCKS, EDGE))

        ids = lax.broadcasted_iota(jnp.int32, (BLOCKS, CAP), 0)
        low = jnp.sum(jnp.where(list_vec[0:1, :] == ids, 1.0, 0.0), axis=1, keepdims=True)
        high = jnp.sum(jnp.where(list_vec[1:2, :] == ids, 1.0, 0.0), axis=1, keepdims=True)
        slot = column_of(slot_vec[...].astype(F32))
        spread = jnp.where(slot == lane.astype(F32), weight, 0.0)
        slot_weight_ref[...] = jnp.zeros_like(slot_weight_ref)
        slot_weight_ref[0:1, :] = jnp.sum(spread * (1.0 - low - high), axis=0, keepdims=True)
        slot_weight_ref[1:2, :] = jnp.sum(spread * low, axis=0, keepdims=True)
        slot_weight_ref[2:3, :] = jnp.sum(spread * high, axis=0, keepdims=True)

        def clear(j, carry):
            place[j] = -1
            for k in range(3):
                index_ref[k, j] = 0
            return carry

        lax.fori_loop(0, BLOCKS, clear, 0)

        def mark(t, carry):
            for side in range(2):
                j = list_ref[side, t]

                @pl.when(j >= 0)
                def leaves():
                    place[j] = side * CAP + t
                    index_ref[1 + side, slot_ref[0, j]] = (5 - side) * CAP + t + 1

            return carry

        lax.fori_loop(0, CAP, mark, 0)

        def fill(j, free):
            stays = place[j] < 0

            @pl.when(stays)
            def keep():
                place[j] = free
                index_ref[0, slot_ref[0, j]] = free + 1

            after = free + stays.astype(jnp.int32)
            return jnp.where((patch == 0) & (after == CAP), 2 * CAP, after)

        first_free = jnp.where(patch == 0, 0, jnp.where(patch == last, CAP, 2 * CAP))
        lax.fori_loop(0, BLOCKS, fill, first_free)

    down = lax.broadcasted_iota(jnp.int32, (EDGE, EDGE), 0)
    across = lax.broadcasted_iota(jnp.int32, (EDGE, EDGE), 1)
    near = jnp.abs(down - across) < EDGE // 2

    def band(taps_ref, j):
        taps = jnp.broadcast_to(taps_ref[pl.ds(j, 1), :], (EDGE, EDGE))
        rolled = pltpu.roll(taps, 0, 1, stride=1, stride_axis=0)
        return jnp.where(near, rolled, 0.0).astype(BF16)

    for local in range(GROUP):
        j = step * GROUP + local
        first = jnp.dot(band(row_taps, j), blocks_ref[local], preferred_element_type=F32)
        warped = jnp.dot(first.astype(BF16), band(col_taps, j), preferred_element_type=F32)
        scaled = warped.astype(BF16).astype(F32) * weights[pl.ds(j, 1), :]
        own_ref[place[j]] = scaled.astype(BF16)


def whole(shape, space=pltpu.VMEM):
    zeros = (0,) * len(shape)
    return pl.BlockSpec(shape, lambda *_: zeros, memory_space=space)


def warp(blocks, send_list, block_slot, block_offset, block_frac, inv_var):
    return pl.pallas_call(
        warp_kernel,
        grid=(BLOCKS // GROUP,),
        out_shape=(
            jax.ShapeDtypeStruct((BLOCKS, EDGE, EDGE), BF16),
            jax.ShapeDtypeStruct((8, EDGE), jnp.int32),
            jax.ShapeDtypeStruct((8, EDGE), F32),
        ),
        in_specs=[
            whole((2, CAP), pltpu.SMEM),
            whole((1, BLOCKS), pltpu.SMEM),
            whole((2, CAP)),
            whole((1, BLOCKS)),
            whole((BLOCKS, 2)),
            whole((BLOCKS, 2)),
            whole((1, BLOCKS)),
            pl.BlockSpec((GROUP, EDGE, EDGE), lambda g: (g, 0, 0)),
        ],
        out_specs=(
            whole((BLOCKS, EDGE, EDGE)),
            whole((8, EDGE), pltpu.SMEM),
            whole((8, EDGE)),
        ),
        scratch_shapes=[
            pltpu.VMEM((BLOCKS, EDGE), F32),
            pltpu.VMEM((BLOCKS, EDGE), F32),
            pltpu.VMEM((BLOCKS, EDGE), F32),
            pltpu.SMEM((BLOCKS,), jnp.int32),
        ],
        compiler_params=pltpu.CompilerParams(vmem_limit_bytes=32 << 20),
        name="warp",
    )(
        send_list,
        block_slot,
        send_list,
        block_slot,
        block_offset,
        block_frac,
        inv_var,
        blocks,
    )


def remote(src, dst, send_sem, recv_sem, **target):
    return pltpu.make_async_remote_copy(
        src_ref=src,
        dst_ref=dst,
        send_sem=send_sem,
        recv_sem=recv_sem,
        device_id=target,
        device_id_type=pl.DeviceIdType.MESH,
    )


def route_kernel(
    own_ref,
    index_ref,
    weight_ref,
    image_ref,
    weight_sum_ref,
    held,
    index_in,
    weight_in,
    index_sum,
    index_flat,
    halo_in,
    send_sem,
    recv_sem,
    local_sem,
):
    me = lax.axis_index("patch")
    last = lax.axis_size("patch") - 1
    has_low, has_high = me > 0, me < last
    low, high = jnp.maximum(me - 1, 0), jnp.minimum(me + 1, last)
    sides = ((has_low, low), (has_high, high))

    barrier = pltpu.get_barrier_semaphore()
    for there, neighbour in sides:

        @pl.when(there)
        def greet():
            pl.semaphore_signal(
                barrier, inc=1, device_id={"patch": neighbour}, device_id_type=pl.DeviceIdType.MESH
            )

    pl.semaphore_wait(barrier, has_low.astype(jnp.int32) + has_high.astype(jnp.int32))

    def copy_of(kind, side, neighbour):
        lands = 1 - side
        pair = (
            (index_ref, index_in.at[lands]),
            (weight_ref, weight_in.at[lands]),
            (own_ref.at[pl.ds(side * CAP, CAP)], held.at[pl.ds((4 + lands) * CAP, CAP)]),
        )[kind]
        return remote(*pair, send_sem.at[side, kind], recv_sem.at[lands, kind], patch=neighbour)

    def halo_copy(side, neighbour):
        lands = 1 - side
        first = HALO if side == 0 else ROWS
        return remote(
            image_ref.at[:, pl.ds(first, HALO)],
            halo_in.at[lands],
            send_sem.at[side, 3],
            recv_sem.at[lands, 3],
            patch=neighbour,
        )

    for side, (there, neighbour) in enumerate(sides):

        @pl.when(there)
        def send():
            for kind in range(3):
                copy_of(kind, side, neighbour).start()

    stay = pltpu.make_async_copy(own_ref, held.at[pl.ds(0, BLOCKS)], local_sem.at[0])
    stay.start()

    for side, (there, neighbour) in enumerate(sides):

        @pl.when(jnp.logical_not(there))
        def nothing():
            index_in[side] = jnp.zeros((8, EDGE), jnp.int32)
            weight_in[side] = jnp.zeros((8, EDGE), F32)
            halo_in[side] = jnp.zeros((SLOT_COLS, HALO, EDGE), BF16)

    for side, (there, neighbour) in enumerate(sides):

        @pl.when(there)
        def arrive():
            for kind in range(2):
                copy_of(kind, 1 - side, neighbour).wait_recv()

    index_sum[...] = jnp.zeros((8, EDGE), jnp.int32)
    found = index_ref[0:1, :] + index_in[0, 2:3, :] + index_in[1, 1:2, :]
    index_sum[0:1, :] = jnp.maximum(found, 1) - 1
    weight_sum_ref[...] = jnp.zeros((8, EDGE), F32)
    weight_sum_ref[0:1, :] = weight_ref[0:1, :] + weight_in[0, 2:3, :] + weight_in[1, 1:2, :]
    flat = pltpu.make_async_copy(index_sum, index_flat, local_sem.at[1])
    flat.start()
    flat.wait()
    stay.wait()
    for side, (there, neighbour) in enumerate(sides):

        @pl.when(there)
        def arrive_blocks():
            copy_of(2, 1 - side, neighbour).wait_recv()

    def put(slot_row, carry):
        for slot_col in range(SLOT_COLS):
            source = index_flat[0, slot_row * SLOT_COLS + slot_col]
            top = pl.multiple_of(HALO + slot_row * EDGE, HALO)
            image_ref[slot_col, pl.ds(top, EDGE), :] = held[source]
        return carry

    lax.fori_loop(0, SLOT_ROWS, put, 0)

    for side, (there, neighbour) in enumerate(sides):

        @pl.when(there)
        def send_halo():
            halo_copy(side, neighbour).start()

    for side, (there, neighbour) in enumerate(sides):

        @pl.when(there)
        def arrive_halo():
            halo_copy(1 - side, neighbour).wait_recv()

    image_ref[:, 0:HALO, :] = halo_in[0]
    image_ref[:, HALO + ROWS : EXT_ROWS, :] = halo_in[1]

    for side, (there, neighbour) in enumerate(sides):

        @pl.when(there)
        def sent():
            for kind in range(3):
                copy_of(kind, side, neighbour).wait_send()
            halo_copy(side, neighbour).wait_send()


def route(own, index, slot_weight):
    vmem = pl.BlockSpec(memory_space=pltpu.VMEM)
    return pl.pallas_call(
        route_kernel,
        out_shape=(
            jax.ShapeDtypeStruct((SLOT_COLS, EXT_ROWS, EDGE), BF16),
            jax.ShapeDtypeStruct((8, EDGE), F32),
        ),
        in_specs=[pl.BlockSpec(memory_space=pl.ANY), vmem, vmem],
        out_specs=(vmem, vmem),
        scratch_shapes=[
            pltpu.VMEM((6 * CAP, EDGE, EDGE), BF16),
            pltpu.VMEM((2, 8, EDGE), jnp.int32),
            pltpu.VMEM((2, 8, EDGE), F32),
            pltpu.VMEM((8, EDGE), jnp.int32),
            pltpu.SMEM((8, EDGE), jnp.int32),
            pltpu.VMEM((2, SLOT_COLS, HALO, EDGE), BF16),
            pltpu.SemaphoreType.DMA((2, 4)),
            pltpu.SemaphoreType.DMA((2, 4)),
            pltpu.SemaphoreType.DMA((2,)),
        ],
        compiler_params=pltpu.CompilerParams(
            collective_id=0, has_side_effects=True, vmem_limit_bytes=32 << 20
        ),
        name="route",
    )(own, index, slot_weight)


def pieces_of(tile):
    found, column = [], tile * EDGE
    while column < (tile + 1) * EDGE:
        window, lane = divmod(column, OUT_WIN)
        count = min(OUT_WIN - lane, (tile + 1) * EDGE - column)
        found.append((window, lane, column - tile * EDGE, count))
        column += count
    return found


def blur_kernel(image_ref, psf_ref, part_ref, wide, windows, taps, acc):
    lane = lax.broadcasted_iota(jnp.int32, (SEGS, EDGE), 1)
    source = lax.broadcasted_iota(jnp.int32, (KSIZE, EDGE), 0)
    target = lax.broadcasted_iota(jnp.int32, (KSIZE, EDGE), 1)
    flip = jnp.where((target + source) % EDGE == 0, 1.0, 0.0).astype(BF16)
    flipped = jnp.dot(psf_ref[...].astype(BF16), flip, preferred_element_type=F32)
    for t in range(STEPS):
        for row_in in range(2):
            for row_out in range(2):
                tap_row = 2 * t + row_in - row_out
                here = (
                    slice(t * 256 + row_in * EDGE, t * 256 + (row_in + 1) * EDGE),
                    slice(row_out * EDGE, (row_out + 1) * EDGE),
                )
                if 0 <= tap_row < KSIZE:
                    spread = jnp.broadcast_to(flipped[tap_row : tap_row + 1, :], (EDGE, EDGE))
                    taps[here] = pltpu.roll(spread, 0, 1, stride=1, stride_axis=0).astype(BF16)
                else:
                    taps[here] = jnp.zeros((EDGE, EDGE), BF16)

    def widen(r, carry):
        rows = pl.ds(pl.multiple_of(r * 32, 32), 32)
        wide[:, rows, :] = image_ref[:, rows, :].astype(F32)
        return carry

    lax.fori_loop(0, EXT_ROWS // 32, widen, 0)

    nothing = jnp.zeros((SEGS, EDGE), F32)

    def spread_rows(g, carry):
        for row_in in range(2):
            start = 2 * g + (HALO - REACH) + row_in
            tiles = [
                wide[i, pl.ds(start, SEGS, stride=SEG_ROWS), :]
                for i in range(SLOT_COLS)
            ]
            for j in range(WINDOWS):
                tile, off = divmod(OUT_WIN * j - REACH, EDGE)
                left = tiles[tile] if tile >= 0 else nothing
                right = tiles[tile + 1] if tile + 1 < SLOT_COLS else nothing
                if off:
                    left = pltpu.roll(left, EDGE - off, 1) if tile >= 0 else nothing
                    right = pltpu.roll(right, EDGE - off, 1) if tile + 1 < SLOT_COLS else nothing
                    left = jnp.where(lane < EDGE - off, left, right)
                windows[j, g, :, row_in * EDGE : (row_in + 1) * EDGE] = left.astype(BF16)
        return carry

    lax.fori_loop(0, EXT_PAIRS, spread_rows, 0)

    def one_window(j, carry):
        lhs = jnp.concatenate(
            [windows[j, t : t + PAIRS].reshape(PAIRS * SEGS, 256) for t in range(STEPS)], axis=1
        )
        acc[j] = jnp.dot(lhs, taps[...], preferred_element_type=F32)
        return carry

    lax.fori_loop(0, WINDOWS, one_window, 0)

    across = lax.broadcasted_iota(jnp.int32, (SEGS, EDGE), 1)

    def gather_tiles(g, carry):
        rows = pl.ds(pl.multiple_of(g * SEGS, SEGS), SEGS)
        for row_out in range(2):
            lanes = slice(row_out * EDGE, (row_out + 1) * EDGE)
            for tile in range(SLOT_COLS):
                total = None
                for window, there, here, count in pieces_of(tile):
                    value = acc[window, rows, lanes]
                    if here != there:
                        value = pltpu.roll(value, (here - there) % EDGE, 1)
                    total = value if total is None else jnp.where(across >= here, value, total)
                part_ref[tile, pl.ds(pl.multiple_of(row_out * (ROWS // 2) + g * SEGS, SEGS), SEGS), :] = (
                    total.astype(BF16)
                )
        return carry

    lax.fori_loop(0, PAIRS, gather_tiles, 0)


def blur(image, psf):
    vmem = pl.BlockSpec(memory_space=pltpu.VMEM)
    return pl.pallas_call(
        blur_kernel,
        out_shape=jax.ShapeDtypeStruct((SLOT_COLS, ROWS, EDGE), BF16),
        in_specs=[vmem, vmem],
        out_specs=vmem,
        scratch_shapes=[
            pltpu.VMEM((SLOT_COLS, EXT_ROWS, EDGE), F32),
            pltpu.VMEM((WINDOWS, EXT_PAIRS, SEGS, 256), BF16),
            pltpu.VMEM((STEPS * 256, 256), BF16),
            pltpu.VMEM((WINDOWS, PAIRS * SEGS, 256), F32),
        ],
        compiler_params=pltpu.CompilerParams(vmem_limit_bytes=48 << 20),
        name="blur",
    )(image, psf)


def reduce_kernel(
    part_ref,
    weight_ref,
    out_ref,
    pair_in,
    pair_sum,
    chip_in,
    weight_in,
    pair_send,
    pair_recv,
    chip_send,
    chip_recv,
    weight_send,
    weight_recv,
):
    me = lax.axis_index("visit")
    count = lax.axis_size("visit")
    chips = count // 2
    chip, core = me // 2, lax.rem(me, 2)
    partner = me + 1 - 2 * core

    barrier = pltpu.get_barrier_semaphore()
    for d in range(1, count):
        pl.semaphore_signal(
            barrier, inc=1, device_id={"visit": lax.rem(me + d, count)}, device_id_type=pl.DeviceIdType.MESH
        )
    pl.semaphore_wait(barrier, count - 1)

    def pair_copy(d):
        other = lax.rem(chip + d, chips)
        return remote(
            part_ref.at[2 * other + 1 - core], pair_in.at[d], pair_send.at[d], pair_recv.at[d], visit=partner
        )

    def chip_copy(d):
        other = lax.rem(chip + d, chips)
        return remote(
            pair_sum.at[d - 1],
            chip_in.at[d - 1],
            chip_send.at[d - 1],
            chip_recv.at[d - 1],
            visit=2 * other + core,
        )

    def weight_copy(d):
        return remote(
            weight_ref,
            weight_in.at[d - 1],
            weight_send.at[d - 1],
            weight_recv.at[d - 1],
            visit=lax.rem(me + d, count),
        )

    order = [2, 1, 3, 0]
    for d in order:
        pair_copy(d).start()
    for d in range(1, count):
        weight_copy(d).start()

    for d in order[:-1]:
        other = lax.rem(chip + d, chips)
        pair_copy(d).wait_recv()

        def add(r, carry):
            rows = pl.ds(pl.multiple_of(r * 128, 128), 128)
            total = part_ref[2 * other + core, rows, :].astype(F32) + pair_in[d, rows, :].astype(F32)
            pair_sum[d - 1, rows, :] = total.astype(BF16)
            return carry

        lax.fori_loop(0, ROWS // 128, add, 0)
        chip_copy(d).start()

    for d in range(1, count):
        weight_copy(d).wait_recv()
    denom = weight_ref[0:1, :]
    for d in range(1, count):
        denom = denom + weight_in[d - 1, 0:1, :]
    lane = lax.broadcasted_iota(jnp.int32, (SEGS, EDGE), 1)
    row = lax.broadcasted_iota(jnp.int32, (SEGS, EDGE), 0)
    wanted = (row // 2) * SLOT_COLS + me
    denom = jnp.sum(jnp.where(lane == wanted, jnp.broadcast_to(denom, (SEGS, EDGE)), 0.0), axis=1, keepdims=True)
    denom = jnp.broadcast_to(denom, (SEGS, EDGE))

    pair_copy(0).wait_recv()
    for d in (1, 3, 2):
        chip_copy(d).wait_recv()

    def finish(g, carry):
        for row_out in range(2):
            rows = pl.ds(pl.multiple_of(row_out * (ROWS // 2) + g * SEGS, SEGS), SEGS)
            total = part_ref[me, rows, :].astype(F32) + pair_in[0, rows, :].astype(F32)
            for d in range(1, chips):
                total = total + chip_in[d - 1, rows, :].astype(F32)
            out_ref[pl.ds(2 * g + row_out, SEGS, stride=SEG_ROWS), :] = total / denom
        return carry

    lax.fori_loop(0, PAIRS, finish, 0)

    for d in order:
        pair_copy(d).wait_send()
    for d in range(1, chips):
        chip_copy(d).wait_send()
    for d in range(1, count):
        weight_copy(d).wait_send()


def reduce(part, weight_sum):
    vmem = pl.BlockSpec(memory_space=pltpu.VMEM)
    count = lax.axis_size("visit")
    chips = count // 2
    return pl.pallas_call(
        reduce_kernel,
        out_shape=jax.ShapeDtypeStruct((ROWS, EDGE), F32),
        in_specs=[vmem, vmem],
        out_specs=vmem,
        scratch_shapes=[
            pltpu.VMEM((chips, ROWS, EDGE), BF16),
            pltpu.VMEM((chips - 1, ROWS, EDGE), BF16),
            pltpu.VMEM((chips - 1, ROWS, EDGE), BF16),
            pltpu.VMEM((count - 1, 8, EDGE), F32),
            pltpu.SemaphoreType.DMA((chips,)),
            pltpu.SemaphoreType.DMA((chips,)),
            pltpu.SemaphoreType.DMA((chips - 1,)),
            pltpu.SemaphoreType.DMA((chips - 1,)),
            pltpu.SemaphoreType.DMA((count - 1,)),
            pltpu.SemaphoreType.DMA((count - 1,)),
        ],
        compiler_params=pltpu.CompilerParams(
            collective_id=1, has_side_effects=True, vmem_limit_bytes=32 << 20
        ),
        name="reduce",
    )(part, weight_sum)


def on_device(blocks, send_list, block_slot, block_offset, block_frac, inv_var, psf_kernel):
    own, index, slot_weight = warp(
        blocks[0], send_list[0, 0], block_slot, block_offset[0], block_frac[0], inv_var
    )
    image, weight_sum = route(own, index, slot_weight)
    part = blur(image, psf_kernel[0])
    return reduce(part, weight_sum)


def solution(mesh):
    in_specs = (
        P("visit", "patch", None, None),
        P("visit", "patch", None, None),
        P("visit", "patch"),
        P("visit", "patch", None),
        P("visit", "patch", None),
        P("visit", "patch"),
        P("visit", None, None),
    )
    out_specs = P("patch", "visit")
    return jax.shard_map(
        on_device, mesh=mesh, in_specs=in_specs, out_specs=out_specs, check_vma=False
    )
```

time: 526 us -> 80 us (0.15)
  matrix products: 299 us -> 0 us
  local copies, waits for them, and re-layouts: 102 us -> 5.91 us
  Pallas kernels: 0 us -> 73.6 us
  waiting for transfers between devices: 57.4 us -> 0 us
  blocking collectives: 24.3 us -> 0 us
  starting transfers between devices: 17.8 us -> 0 us
  between operations: 13.7 us -> 0.05 us
  other arithmetic: 10.5 us -> 0 us
    dot_general x29 -> x0, matrix products: 299 us -> none  [the longest x25 195 us: add_row(): jnp.einsum('rtk,kc->rtc', row_band, row_taps, preferred_element_type=jnp....]
    gather x6 -> x0, local copies, waits for them, and re-layouts: 74.3 us -> none  [the longest x2 72.3 us: on_device(): kernel[:, jnp.clip(tap_lag, 0, KSIZE - 1)]]
    pallas_call x0 -> x4, Pallas kernels: none -> 73.6 us  [the longest x1 24.4 us: route(): pl.pallas_call(route_kernel, out_shape=(jax.ShapeDtypeStruct((SLOT_COLS,...]
    psum x1 -> x0, waiting for transfers between devices: 53.3 us -> none  [on_device(): numer_all, denom_all = lax.psum((blurred, denom_cols), 'visit')]
    psum x1 -> x0, blocking collectives: 24.3 us -> none  [on_device(): numer_all, denom_all = lax.psum((blurred, denom_cols), 'visit')]
    ppermute x4 -> x0, starting transfers between devices: 17.8 us -> none  [the longest x2 12.1 us: extended(): lax.ppermute(lax.slice_in_dim(block, 0, width, axis=dim), axis, backward)]
    concatenate x4 -> x0, local copies, waits for them, and re-layouts: 6.83 us -> none  [the longest x1 5.41 us: extended(): block = jnp.concatenate([low, block, high], axis=dim)]
  transfers between devices with their start and end apart: 5 -> 0, of which waited for: 3 -> 0; matrix products, arithmetic and copies ran while one was open for 27% -> 0% of each run, Pallas kernels for 0% -> 0%
where the time goes in v1:
time: 80 us; the launch traced here: 79.6 us
  Pallas kernels  73.6 us (92%)
  local copies, waits for them, and re-layouts  5.91 us (7%)
    pallas_call x1, Pallas kernels, route(): pl.pallas_call(route_kernel, out_shape=(jax.ShapeDtypeStruct((SLOT_COLS,...  24.4 us
    pallas_call x1, Pallas kernels, blur(): pl.pallas_call(blur_kernel, out_shape=jax.ShapeDtypeStruct((SLOT_COLS, RO...  23.1 us
    pallas_call x1, Pallas kernels, reduce(): pl.pallas_call(reduce_kernel, out_shape=jax.ShapeDtypeStruct((ROWS, EDGE)...  19.2 us
    pallas_call x1, Pallas kernels, warp(): pl.pallas_call(warp_kernel, grid=(BLOCKS // GROUP,), out_shape=(jax.Shape...  6.87 us
    unnamed x12, local copies, waits for them, and re-layouts  4.38 us

profile of v1, /device:TPU:24, one launch (start us, length us, event | category | flops | bytes accessed | tf_op | source)
XLA Modules:
  0.0 79.6 jit_solution(8696630445569759804)
XLA Ops:
  0.0 0.8 copy.8.offset_ref
  0.8 0.8 copy.9.frac_ref
  1.5 0.0 copy-start
  1.5 1.6 %copy-done = bf16[1,64,128,128]{3,2,1,0:T(8,128)(2,1)S(1)} copy-done((bf16[1,64,128,128]{3,2,1,0:T(8,128)(2,1)S(1)}, bf16[1,64,128,128]{3,2,1,0:T(8,128)(2,1)}, u32[]{:S(2)}) %copy-start) | copy-done | bytes 2097176
  3.1 0.0 copy-start.1
  3.1 0.7 copy-done.1
  3.8 0.0 copy-start.2
  3.8 0.7 copy-done.2
  4.5 0.0 copy-start.3
  4.5 0.7 copy-done.3
  5.1 0.0 copy-start.4
  5.1 6.9 %warp.1 = (bf16[64,128,128]{2,1,0:T(8,128)(2,1)S(1)}, s32[8,128]{1,0:T(8,128)S(1)}, f32[8,128]{1,0:T(8,128)S(1)}) custom-call(s32[2,16]{1,0:T(2,128)S(1)} %bitcast.9, s32[1,64]{1,0:T(1,128)S(1)} %copy-done.2, s32[2,16]{1,0:T(2,128)S(1)} %bitcast.10, s32[1,64]{1,0:T(1,128)S(1)} %copy-done.2, s32[64,2]{1,0:T(8,128)S(1)} %copy.8.offset_ref, ...), custom_call_target="tpu_custom_call" | custom-call | tf_op jit(solution)/shard_map/warp/pallas_call | solution.py:152
  12.0 24.4 %route.1 = (bf16[8,1056,128]{2,1,0:T(8,128)(2,1)S(1)}, f32[8,128]{1,0:T(8,128)S(1)}) custom-call(bf16[64,128,128]{2,1,0:T(8,128)(2,1)S(1)} %get-tuple-element.10.own_ref, s32[8,128]{1,0:T(8,128)S(1)} %get-tuple-element.11.index_ref, f32[8,128]{1,0:T(8,128)S(1)} %get-tuple-element.12.weight_ref), custom_call_target="tpu_custom_call" | custom-call | tf_op jit(solution)/shard_map/route/pallas_call | solution.py:334
  36.4 0.0 copy-done.4
  36.4 23.1 %blur.1.part_ref = bf16[8,1024,128]{2,1,0:T(8,128)(2,1)S(1)} custom-call(bf16[8,1056,128]{2,1,0:T(8,128)(2,1)S(1)} %get-tuple-element.13.image_ref, f32[25,25]{1,0:T(8,128)S(1)} %bitcast.8), custom_call_target="tpu_custom_call" | custom-call | tf_op jit(solution)/shard_map/blur/pallas_call | solution.py:451
  59.5 19.2 %reduce.1 = f32[1024,128]{1,0:T(8,128)S(1)} custom-call(bf16[8,1024,128]{2,1,0:T(8,128)(2,1)S(1)} %blur.1.part_ref, f32[8,128]{1,0:T(8,128)S(1)} %get-tuple-element.14.weight_ref), custom_call_target="tpu_custom_call" | custom-call | tf_op jit(solution)/shard_map/reduce/pallas_call | solution.py:577
  78.8 0.8 %copy.14 = f32[1024,128]{1,0:T(8,128)} copy(f32[1024,128]{1,0:T(8,128)S(1)} %reduce.1) | data formatting | bytes 1048576
  (1 shorter events, 0.0 us)
Async XLA Ops:
  1.5 1.6 %copy-start = (bf16[1,64,128,128]{3,2,1,0:T(8,128)(2,1)S(1)}, bf16[1,64,128,128]{3,2,1,0:T(8,128)(2,1)}, u32[]{:S(2)}) copy-start(bf16[1,64,128,128]{3,2,1,0:T(8,128)(2,1)} %param.7) | copy-start | bytes 6291460
  3.1 0.7 copy-start.1
  3.8 0.7 copy-start.2
  4.5 0.7 copy-start.3
  5.1 31.3 %copy-start.4 = (f32[1,25,25]{2,0,1:T(1,128)S(1)}, f32[1,25,25]{2,0,1:T(1,128)}, u32[]{:S(2)}) copy-start(f32[1,25,25]{2,0,1:T(1,128)} %param.13) | copy-start | bytes 7504

commit v2 on v0

v2 whole, which is shorter than its diff:
```python
import math

import jax
import jax.numpy as jnp
from jax import lax
from jax.experimental import pallas as pl
from jax.experimental.pallas import tpu as pltpu
from jax.sharding import PartitionSpec as P

EDGE = 128
BLOCKS = 64
CAP = 16
KSIZE = 25
REACH = 12
GROUP = 8
CHUNK = 4
SLOT_COLS = 8
SLOT_ROWS = 8
ROWS = SLOT_ROWS * EDGE
COLS = SLOT_COLS * EDGE
HALO = 16
EXT_ROWS = ROWS + 2 * HALO
SEGS = 16
SEG_ROWS = ROWS // SEGS
PAIRS = SEG_ROWS // 2
STEPS = KSIZE // 2 + 1
EXT_PAIRS = PAIRS + STEPS - 1
SIDE = 2 * REACH
PACK = EDGE // SIDE
HALVES = -(-2 * STEPS // PACK)
DEPTH = STEPS * 2 * EDGE + HALVES * EDGE
TILE_ROWS = PAIRS * SEGS
F32 = jnp.float32
BF16 = jnp.bfloat16


def lanczos_weight(tap_offset):
    inside = jnp.abs(tap_offset) < 3.0
    safe_tap = jnp.where(inside, tap_offset, 1.5)
    value = (
        3.0
        * jnp.sin(math.pi * safe_tap)
        * jnp.sin(math.pi * safe_tap / 3.0)
        / (math.pi * math.pi * safe_tap * safe_tap)
    )
    return jnp.where(inside, value, 0.0)


def column_of(row):
    count = row.shape[1]
    down = lax.broadcasted_iota(jnp.int32, (count, count), 0)
    across = lax.broadcasted_iota(jnp.int32, (count, count), 1)
    spread = jnp.where(down == across, jnp.broadcast_to(row, (count, count)), 0.0)
    return jnp.sum(spread, axis=1, keepdims=True)


def toeplitz(row, rows):
    return pltpu.roll(jnp.broadcast_to(row, (rows, EDGE)), 0, 1, stride=1, stride_axis=0)


def build_taps(psf_ref, psf_rows, taps):
    for a in range(KSIZE):
        psf_rows[a : a + 1, :] = psf_ref[a]
    source = lax.broadcasted_iota(jnp.int32, (KSIZE, EDGE), 0)
    target = lax.broadcasted_iota(jnp.int32, (KSIZE, EDGE), 1)
    flip = jnp.where((target + source) % EDGE == 0, 1.0, 0.0).astype(BF16)
    flipped = jnp.dot(psf_rows[...].astype(BF16), flip, preferred_element_type=F32)
    centred = pltpu.roll(flipped, REACH, 1)
    down = lax.broadcasted_iota(jnp.int32, (EDGE, EDGE), 0)
    across = lax.broadcasted_iota(jnp.int32, (EDGE, EDGE), 1)
    near = jnp.abs(across - down) <= REACH
    beside = (down[:SIDE] < REACH) == (across[:SIDE] < EDGE // 2)

    def lanes(row_out):
        return slice(row_out * EDGE, (row_out + 1) * EDGE)

    for a in range(-1, KSIZE + 1):
        if 0 <= a < KSIZE:
            block = jnp.where(near, toeplitz(centred[a : a + 1], EDGE), 0.0).astype(BF16)
        else:
            block = jnp.zeros((EDGE, EDGE), BF16)
        for row_out in range(2):
            row_in = a + row_out
            if 0 <= row_in < 2 * STEPS:
                taps[row_in * EDGE : (row_in + 1) * EDGE, lanes(row_out)] = block
    for half in range(HALVES):
        for row_out in range(2):
            parts = []
            for i in range(PACK):
                a = PACK * half + i - row_out
                if 0 <= a < KSIZE:
                    parts.append(jnp.where(beside, toeplitz(flipped[a : a + 1], SIDE), 0.0))
                else:
                    parts.append(jnp.zeros((SIDE, EDGE), F32))
            parts.append(jnp.zeros((EDGE - PACK * SIDE, EDGE), F32))
            base = STEPS * 2 * EDGE + half * EDGE
            taps[base : base + EDGE, lanes(row_out)] = jnp.concatenate(parts, axis=0).astype(BF16)


def build_select(select):
    shape = (4 * EDGE, 2 * EDGE)
    source = lax.broadcasted_iota(jnp.int32, shape, 0)
    lane = lax.broadcasted_iota(jnp.int32, shape, 1)
    inner = lax.rem(lane, EDGE)
    q = lax.rem(inner, SIDE)
    wanted = jnp.where(q < REACH, EDGE - REACH + q, 2 * EDGE + q - REACH) + (lane - inner)
    hit = (source == wanted) & (inner < PACK * SIDE)
    select[...] = jnp.where(hit, 1.0, 0.0).astype(BF16)


def remote(src, dst, send_sem, recv_sem, **target):
    return pltpu.make_async_remote_copy(
        src_ref=src,
        dst_ref=dst,
        send_sem=send_sem,
        recv_sem=recv_sem,
        device_id=target,
        device_id_type=pl.DeviceIdType.MESH,
    )


def coadd_kernel(
    list_hbm,
    slot_hbm,
    offset_hbm,
    frac_hbm,
    inv_var_hbm,
    psf_hbm,
    blocks_hbm,
    out_ref,
    lists,
    slots,
    slot_vec,
    offset_vec,
    frac_vec,
    inv_var_vec,
    psf_vec,
    psf_rows,
    raw,
    row_taps,
    col_taps,
    weights,
    staying,
    staying_flat,
    index_mine,
    index_in,
    index_sum,
    index_flat,
    weight_mine,
    weight_in,
    weight_sum,
    weight_all,
    outgoing,
    held,
    wide,
    halo_out,
    halo_in,
    centre,
    edges,
    sides,
    select,
    taps,
    own_part,
    pair_out,
    pair_in,
    relay_out,
    relay_in,
    chip_out,
    chip_in,
    local_sem,
    block_send,
    block_recv,
    meta_send,
    meta_recv,
    halo_send,
    halo_recv,
    pair_send,
    pair_recv,
    relay_send,
    relay_recv,
    chip_send,
    chip_recv,
    weight_send,
    weight_recv,
):
    patch = lax.axis_index("patch")
    last = lax.axis_size("patch") - 1
    visit = lax.axis_index("visit")
    visits = lax.axis_size("visit")
    chips = visits // 2
    chip, core = visit // 2, lax.rem(visit, 2)
    partner = visit + 1 - 2 * core
    has_low, has_high = patch > 0, patch < last
    sides_of = (
        (has_low, jnp.maximum(patch - 1, 0)),
        (has_high, jnp.minimum(patch + 1, last)),
    )

    loads = [
        pltpu.make_async_copy(src, dst, local_sem.at[i])
        for i, (src, dst) in enumerate(
            (
                (offset_hbm, offset_vec),
                (frac_hbm, frac_vec),
                (inv_var_hbm, inv_var_vec),
                (list_hbm, lists),
                (slot_hbm, slots),
                (slot_hbm, slot_vec),
                (psf_hbm, psf_vec),
                (blocks_hbm, raw),
            )
        )
    ]
    for load in loads:
        load.start()

    barrier = pltpu.get_barrier_semaphore()
    for there, neighbour in sides_of:

        @pl.when(there)
        def greet():
            pl.semaphore_signal(
                barrier, inc=1, device_id={"patch": neighbour}, device_id_type=pl.DeviceIdType.MESH
            )

    for d in range(1, visits):
        pl.semaphore_signal(
            barrier,
            inc=1,
            device_id={"visit": lax.rem(visit + d, visits)},
            device_id_type=pl.DeviceIdType.MESH,
        )

    for load in loads[:3]:
        load.wait()
    shift_rows = column_of(offset_vec[0:1, :].astype(F32) + frac_vec[0:1, :].astype(F32))
    shift_cols = column_of(offset_vec[1:2, :].astype(F32) + frac_vec[1:2, :].astype(F32))
    lane_block = lax.broadcasted_iota(jnp.int32, (BLOCKS, EDGE), 1)
    signed = jnp.where(lane_block < EDGE // 2, lane_block, lane_block - EDGE).astype(F32)
    row_taps[...] = lanczos_weight(signed - shift_rows).astype(BF16).astype(F32)
    col_taps[...] = lanczos_weight(-signed - shift_cols).astype(BF16).astype(F32)
    weights[...] = jnp.broadcast_to(column_of(inv_var_vec[...].astype(F32)), (BLOCKS, EDGE))

    down = lax.broadcasted_iota(jnp.int32, (EDGE, EDGE), 0)
    across = lax.broadcasted_iota(jnp.int32, (EDGE, EDGE), 1)
    near = jnp.abs(down - across) < EDGE // 2

    def band(taps_ref, j):
        rolled = toeplitz(taps_ref[pl.ds(j, 1), :], EDGE)
        return jnp.where(near, rolled, 0.0).astype(BF16)

    def warped(j):
        first = jnp.dot(band(row_taps, j), raw[j], preferred_element_type=F32)
        second = jnp.dot(first.astype(BF16), band(col_taps, j), preferred_element_type=F32)
        return (second.astype(BF16).astype(F32) * weights[pl.ds(j, 1), :]).astype(BF16)

    def block_copy(side, chunk, neighbour):
        lands = 1 - side
        return remote(
            outgoing.at[side, pl.ds(chunk * CHUNK, CHUNK)],
            held.at[pl.ds(BLOCKS + lands * CAP + chunk * CHUNK, CHUNK)],
            block_send.at[side, chunk],
            block_recv.at[lands, chunk],
            patch=neighbour,
        )

    def meta_copy(side, kind, neighbour):
        lands = 1 - side
        src, dst = ((index_mine, index_in), (weight_mine, weight_in))[kind]
        return remote(
            src, dst.at[lands], meta_send.at[side, kind], meta_recv.at[lands, kind], patch=neighbour
        )

    def halo_copy(side, neighbour):
        lands = 1 - side
        return remote(
            halo_out.at[side], halo_in.at[lands], halo_send.at[side], halo_recv.at[lands], patch=neighbour
        )

    for load in loads[3:]:
        load.wait()
    pl.semaphore_wait(barrier, visits - 1 + has_low.astype(jnp.int32) + has_high.astype(jnp.int32))

    def leave(chunk, carry):
        for side in range(2):
            for i in range(CHUNK):
                t = chunk * CHUNK + i
                outgoing[side, t] = warped(jnp.maximum(lists[side, t], 0))
        for side, (there, neighbour) in enumerate(sides_of):

            @pl.when(there)
            def send():
                block_copy(side, chunk, neighbour).start()

        return carry

    lax.fori_loop(0, CAP // CHUNK, leave, 0)

    lane = lax.broadcasted_iota(jnp.int32, (1, EDGE), 1)

    def list_leaving(t, carry):
        leaving, index_low, index_high, weight_low, weight_high = carry
        found = []
        for side in range(2):
            j = lists[side, t]
            inside = jnp.maximum(j, 0)
            leaving = jnp.where(lane == j, 1, leaving)
            here = (lane == slots[0, inside]) & (jnp.broadcast_to(j, (1, EDGE)) >= 0)
            code = BLOCKS + (1 - side) * CAP + t + 1
            found.append((jnp.where(here, code, 0), jnp.where(here, weights[pl.ds(inside, 1), :], 0.0)))
        return (
            leaving,
            index_low + found[0][0],
            index_high + found[1][0],
            weight_low + found[0][1],
            weight_high + found[1][1],
        )

    zeros_i = jnp.zeros((1, EDGE), jnp.int32)
    zeros_f = jnp.zeros((1, EDGE), F32)
    leaving, index_low, index_high, weight_low, weight_high = lax.fori_loop(
        0, CAP, list_leaving, (zeros_i, zeros_i, zeros_i, zeros_f, zeros_f)
    )
    staying[...] = jnp.full((8, EDGE), EDGE, jnp.int32)
    staying[0:1, 0:BLOCKS] = jnp.where(leaving[:, 0:BLOCKS] > 0, EDGE, slot_vec[...])
    flat = pltpu.make_async_copy(staying, staying_flat, local_sem.at[8])
    flat.start()
    flat.wait()

    def list_staying(j, carry):
        index_own, weight_own = carry
        here = lane == staying_flat[0, j]
        return (
            index_own + jnp.where(here, j + 1, 0),
            weight_own + jnp.where(here, weights[pl.ds(j, 1), :], 0.0),
        )

    index_own, weight_own = lax.fori_loop(0, BLOCKS, list_staying, (zeros_i, zeros_f))
    index_mine[...] = jnp.zeros((8, EDGE), jnp.int32)
    weight_mine[...] = jnp.zeros((8, EDGE), F32)
    for k, (index, weight) in enumerate(
        ((index_own, weight_own), (index_low, weight_low), (index_high, weight_high))
    ):
        index_mine[k : k + 1, :] = index
        weight_mine[k : k + 1, :] = weight
    for side, (there, neighbour) in enumerate(sides_of):

        @pl.when(there)
        def send_meta():
            for kind in range(2):
                meta_copy(side, kind, neighbour).start()

        @pl.when(jnp.logical_not(there))
        def nothing_comes():
            index_in[side] = jnp.zeros((8, EDGE), jnp.int32)
            weight_in[side] = jnp.zeros((8, EDGE), F32)
            halo_in[side] = jnp.zeros((SLOT_COLS, HALO, EDGE), BF16)

    def warp_group(group, carry):
        for i in range(GROUP):
            j = group * GROUP + i
            held[j] = warped(j)
        return carry

    lax.fori_loop(0, BLOCKS // GROUP, warp_group, 0)

    build_taps(psf_vec, psf_rows, taps)
    build_select(select)
    blank = jnp.zeros((EXT_PAIRS, SEGS, 2 * EDGE), BF16)
    centre[0] = blank
    centre[SLOT_COLS + 1] = blank
    edges[EXT_PAIRS : EXT_PAIRS + 2] = jnp.zeros((2, SEGS, 2 * EDGE), F32)

    for side, (there, neighbour) in enumerate(sides_of):

        @pl.when(there)
        def meta_arrives():
            for kind in range(2):
                meta_copy(1 - side, kind, neighbour).wait_recv()

    index_sum[...] = jnp.zeros((8, EDGE), jnp.int32)
    found = index_mine[0:1, :] + index_in[0, 2:3, :] + index_in[1, 1:2, :]
    index_sum[0:1, :] = jnp.clip(found, 1, BLOCKS + 2 * CAP) - 1
    weight_sum[...] = jnp.zeros((8, EDGE), F32)
    weight_sum[0:1, :] = weight_mine[0:1, :] + weight_in[0, 2:3, :] + weight_in[1, 1:2, :]

    def weight_copy(d):
        return remote(
            weight_sum,
            weight_all.at[d - 1],
            weight_send.at[d - 1],
            weight_recv.at[d - 1],
            visit=lax.rem(visit + d, visits),
        )

    for d in range(1, visits):
        weight_copy(d).start()
    flat = pltpu.make_async_copy(index_sum, index_flat, local_sem.at[9])
    flat.start()
    flat.wait()
    for side, (there, neighbour) in enumerate(sides_of):

        @pl.when(there)
        def blocks_arrive():
            for chunk in range(CAP // CHUNK):
                block_copy(1 - side, chunk, neighbour).wait_recv()

    def put(slot_row, carry):
        for slot_col in range(SLOT_COLS):
            source = index_flat[0, slot_row * SLOT_COLS + slot_col]
            top = pl.multiple_of(HALO + slot_row * EDGE, HALO)
            wide[slot_col, pl.ds(top, EDGE), :] = held[source].astype(F32)
        return carry

    lax.fori_loop(0, 2, lambda i, carry: put(i * (SLOT_ROWS - 1), carry), 0)
    halo_out[0] = wide[:, HALO : 2 * HALO, :].astype(BF16)
    halo_out[1] = wide[:, ROWS : ROWS + HALO, :].astype(BF16)
    for side, (there, neighbour) in enumerate(sides_of):

        @pl.when(there)
        def send_halo():
            halo_copy(side, neighbour).start()

    lax.fori_loop(1, SLOT_ROWS - 1, put, 0)

    def to_pairs(g, carry):
        for row_in in range(2):
            start = 2 * g + (HALO - REACH) + row_in
            for w in range(SLOT_COLS):
                rows = wide[w, pl.ds(start, SEGS, stride=SEG_ROWS), :]
                centre[w + 1, g, :, row_in * EDGE : (row_in + 1) * EDGE] = rows.astype(BF16)
        return carry

    lax.fori_loop(REACH // 2, REACH // 2 + PAIRS, to_pairs, 0)
    for side, (there, neighbour) in enumerate(sides_of):

        @pl.when(there)
        def halo_arrives():
            halo_copy(1 - side, neighbour).wait_recv()

    wide[:, 0:HALO, :] = halo_in[0].astype(F32)
    wide[:, HALO + ROWS : EXT_ROWS, :] = halo_in[1].astype(F32)
    lax.fori_loop(0, REACH // 2, to_pairs, 0)
    lax.fori_loop(REACH // 2 + PAIRS, EXT_PAIRS, to_pairs, 0)

    lane_seg = lax.broadcasted_iota(jnp.int32, (SEGS, EDGE), 1)

    def side_columns(w, carry):
        both = jnp.concatenate(
            [centre[w + k].reshape(EXT_PAIRS * SEGS, 2 * EDGE) for k in (0, 2)], axis=1
        )
        placed = jnp.dot(both, select[...], preferred_element_type=F32)
        edges[0:EXT_PAIRS] = placed.reshape(EXT_PAIRS, SEGS, 2 * EDGE)

        def pack(i, inner):
            for k in range(4):
                g = i * 4 + k
                rows = [edges[g + n // 2, :, (n % 2) * EDGE : (n % 2 + 1) * EDGE] for n in range(PACK + 1)]
                for odd in range(2):
                    packed = rows[odd + PACK - 1]
                    for n in range(PACK - 2, -1, -1):
                        packed = jnp.where(lane_seg < (n + 1) * SIDE, rows[odd + n], packed)
                    sides[odd, w, g] = packed.astype(BF16)
            return inner

        lax.fori_loop(0, EXT_PAIRS // 4, pack, 0)
        return carry

    lax.fori_loop(0, SLOT_COLS, side_columns, 0)

    def pair_copy(k):
        return remote(pair_out.at[k], pair_in.at[k], pair_send.at[k], pair_recv.at[k], visit=partner)

    ahead = 2 * lax.rem(chip + 1, chips) + core
    behind = 2 * lax.rem(chip + chips - 1, chips) + core
    ways = (ahead, behind)

    def relay_copy(way):
        return remote(
            relay_out.at[way], relay_in.at[way], relay_send.at[way], relay_recv.at[way], visit=ways[way]
        )

    def chip_copy(way):
        return remote(
            chip_out.at[way], chip_in.at[way], chip_send.at[way], chip_recv.at[way], visit=ways[way]
        )

    def total(k, half, r):
        rows = pl.ds(pl.multiple_of(half * TILE_ROWS + r * EDGE, EDGE), EDGE)
        return rows, own_part[rows, :] + pair_in[k, rows, :].astype(F32)

    strips = TILE_ROWS // EDGE

    def tile_step(i, carry):
        k = i // 2
        mine = lax.rem(i, 2)
        distance = jnp.where(k == 0, 2, jnp.where(k == 1, 1, jnp.where(k == 2, chips - 1, 0)))
        to_core = jnp.where(mine == 1, core, 1 - core)
        w = 2 * lax.rem(chip + distance, chips) + to_core
        columns = [
            centre[w + 1, t : t + PAIRS].reshape(TILE_ROWS, 2 * EDGE) for t in range(STEPS)
        ]
        for half in range(HALVES):
            row = PACK * half
            columns.append(sides[row % 2, w, row // 2 : row // 2 + PAIRS].reshape(TILE_ROWS, EDGE))
        acc = jnp.dot(jnp.concatenate(columns, axis=1), taps[...], preferred_element_type=F32)

        @pl.when(mine == 0)
        def for_partner():
            for row_out in range(2):
                pair_out[k, row_out * TILE_ROWS : (row_out + 1) * TILE_ROWS, :] = acc[
                    :, row_out * EDGE : (row_out + 1) * EDGE
                ].astype(BF16)
            pair_copy(k).start()

        @pl.when(mine == 1)
        def for_this_core():
            for row_out in range(2):
                own_part[row_out * TILE_ROWS : (row_out + 1) * TILE_ROWS, :] = acc[
                    :, row_out * EDGE : (row_out + 1) * EDGE
                ]
            pair_copy(k).wait_recv()

            @pl.when(k == 0)
            def opposite():
                for way in range(2):

                    def add(r, inner):
                        _, value = total(k, way, r)
                        relay_out[way, pl.ds(pl.multiple_of(r * EDGE, EDGE), EDGE), :] = value.astype(BF16)
                        return inner

                    lax.fori_loop(0, strips, add, 0)
                    relay_copy(way).start()

            for way in range(2):

                @pl.when(k == 1 + way)
                def beside():
                    relay_copy(way).wait_recv()
                    for half in range(2):

                        def add(r, inner):
                            rows, value = total(k, half, r)
                            if half == way:
                                value = value + relay_in[way, pl.ds(pl.multiple_of(r * EDGE, EDGE), EDGE), :].astype(F32)
                            chip_out[way, rows, :] = value.astype(BF16)
                            return inner

                        lax.fori_loop(0, strips, add, 0)
                    chip_copy(way).start()

        return carry

    lax.fori_loop(0, SLOT_COLS, tile_step, 0)

    for d in range(1, visits):
        weight_copy(d).wait_recv()
    denom = weight_sum[0:1, :]
    for d in range(1, visits):
        denom = denom + weight_all[d - 1, 0:1, :]
    row_seg = lax.broadcasted_iota(jnp.int32, (SEGS, EDGE), 0)
    wanted = (row_seg // 2) * SLOT_COLS + visit
    denom = jnp.sum(
        jnp.where(lane_seg == wanted, jnp.broadcast_to(denom, (SEGS, EDGE)), 0.0), axis=1, keepdims=True
    )
    denom = jnp.broadcast_to(denom, (SEGS, EDGE))
    for way in range(2):
        chip_copy(way).wait_recv()

    def finish(g, carry):
        for row_out in range(2):
            rows = pl.ds(pl.multiple_of(row_out * TILE_ROWS + g * SEGS, SEGS), SEGS)
            value = own_part[rows, :] + pair_in[chips - 1, rows, :].astype(F32)
            for way in range(2):
                value = value + chip_in[way, rows, :].astype(F32)
            out_ref[pl.ds(2 * g + row_out, SEGS, stride=SEG_ROWS), :] = value / denom
        return carry

    lax.fori_loop(0, PAIRS, finish, 0)

    for side, (there, neighbour) in enumerate(sides_of):

        @pl.when(there)
        def sent():
            for chunk in range(CAP // CHUNK):
                block_copy(side, chunk, neighbour).wait_send()
            for kind in range(2):
                meta_copy(side, kind, neighbour).wait_send()
            halo_copy(side, neighbour).wait_send()

    for k in range(chips):
        pair_copy(k).wait_send()
    for way in range(2):
        relay_copy(way).wait_send()
        chip_copy(way).wait_send()
    for d in range(1, visits):
        weight_copy(d).wait_send()


def coadd(send_list, block_slot, block_offset, block_frac, inv_var, psf, blocks):
    visits = lax.axis_size("visit")
    chips = visits // 2
    hbm = pl.BlockSpec(memory_space=pl.ANY)
    dma = pltpu.SemaphoreType.DMA
    return pl.pallas_call(
        coadd_kernel,
        out_shape=jax.ShapeDtypeStruct((ROWS, EDGE), F32),
        in_specs=[hbm] * 7,
        out_specs=pl.BlockSpec(memory_space=pltpu.VMEM),
        scratch_shapes=[
            pltpu.SMEM((2, CAP), jnp.int32),
            pltpu.SMEM((1, BLOCKS), jnp.int32),
            pltpu.VMEM((1, BLOCKS), jnp.int32),
            pltpu.VMEM((2, BLOCKS), jnp.int32),
            pltpu.VMEM((2, BLOCKS), BF16),
            pltpu.VMEM((1, BLOCKS), BF16),
            pltpu.VMEM((KSIZE, 1, KSIZE), F32),
            pltpu.VMEM((KSIZE, KSIZE), F32),
            pltpu.VMEM((BLOCKS, EDGE, EDGE), BF16),
            pltpu.VMEM((BLOCKS, EDGE), F32),
            pltpu.VMEM((BLOCKS, EDGE), F32),
            pltpu.VMEM((BLOCKS, EDGE), F32),
            pltpu.VMEM((8, EDGE), jnp.int32),
            pltpu.SMEM((8, EDGE), jnp.int32),
            pltpu.VMEM((8, EDGE), jnp.int32),
            pltpu.VMEM((2, 8, EDGE), jnp.int32),
            pltpu.VMEM((8, EDGE), jnp.int32),
            pltpu.SMEM((8, EDGE), jnp.int32),
            pltpu.VMEM((8, EDGE), F32),
            pltpu.VMEM((2, 8, EDGE), F32),
            pltpu.VMEM((8, EDGE), F32),
            pltpu.VMEM((visits - 1, 8, EDGE), F32),
            pltpu.VMEM((2, CAP, EDGE, EDGE), BF16),
            pltpu.VMEM((BLOCKS + 2 * CAP, EDGE, EDGE), BF16),
            pltpu.VMEM((SLOT_COLS, EXT_ROWS, EDGE), F32),
            pltpu.VMEM((2, SLOT_COLS, HALO, EDGE), BF16),
            pltpu.VMEM((2, SLOT_COLS, HALO, EDGE), BF16),
            pltpu.VMEM((SLOT_COLS + 2, EXT_PAIRS, SEGS, 2 * EDGE), BF16),
            pltpu.VMEM((EXT_PAIRS + 2, SEGS, 2 * EDGE), F32),
            pltpu.VMEM((2, SLOT_COLS, EXT_PAIRS, SEGS, EDGE), BF16),
            pltpu.VMEM((4 * EDGE, 2 * EDGE), BF16),
            pltpu.VMEM((DEPTH, 2 * EDGE), BF16),
            pltpu.VMEM((ROWS, EDGE), F32),
            pltpu.VMEM((chips, ROWS, EDGE), BF16),
            pltpu.VMEM((chips, ROWS, EDGE), BF16),
            pltpu.VMEM((2, TILE_ROWS, EDGE), BF16),
            pltpu.VMEM((2, TILE_ROWS, EDGE), BF16),
            pltpu.VMEM((2, ROWS, EDGE), BF16),
            pltpu.VMEM((2, ROWS, EDGE), BF16),
            dma((10,)),
            dma((2, CAP // CHUNK)),
            dma((2, CAP // CHUNK)),
            dma((2, 2)),
            dma((2, 2)),
            dma((2,)),
            dma((2,)),
            dma((chips,)),
            dma((chips,)),
            dma((2,)),
            dma((2,)),
            dma((2,)),
            dma((2,)),
            dma((visits - 1,)),
            dma((visits - 1,)),
        ],
        compiler_params=pltpu.CompilerParams(
            collective_id=0, has_side_effects=True, vmem_limit_bytes=56 << 20
        ),
        name="coadd",
    )(send_list, block_slot, block_offset, block_frac, inv_var, psf, blocks)


def on_device(blocks, send_list, block_slot, block_offset, block_frac, inv_var, psf_kernel):
    return coadd(
        send_list[0, 0],
        block_slot,
        block_offset[0].T,
        block_frac[0].T,
        inv_var,
        jnp.transpose(psf_kernel, (1, 0, 2)),
        blocks[0],
    )


def solution(mesh):
    in_specs = (
        P("visit", "patch", None, None),
        P("visit", "patch", None, None),
        P("visit", "patch"),
        P("visit", "patch", None),
        P("visit", "patch", None),
        P("visit", "patch"),
        P("visit", None, None),
    )
    out_specs = P("patch", "visit")
    return jax.shard_map(
        on_device, mesh=mesh, in_specs=in_specs, out_specs=out_specs, check_vma=False
    )
```

time: 526 us -> 54.8 us (0.10)
  matrix products: 299 us -> 0 us
  local copies, waits for them, and re-layouts: 102 us -> 1.87 us
  waiting for transfers between devices: 57.4 us -> 0 us
  Pallas kernels: 0 us -> 52.8 us
  blocking collectives: 24.3 us -> 0 us
  starting transfers between devices: 17.8 us -> 0 us
  between operations: 13.7 us -> 0.01 us
  other arithmetic: 10.5 us -> 0 us
    dot_general x29 -> x0, matrix products: 299 us -> none  [the longest x25 195 us: add_row(): jnp.einsum('rtk,kc->rtc', row_band, row_taps, preferred_element_type=jnp....]
    gather x6 -> x0, local copies, waits for them, and re-layouts: 74.3 us -> none  [the longest x2 72.3 us: on_device(): kernel[:, jnp.clip(tap_lag, 0, KSIZE - 1)]]
    psum x1 -> x0, waiting for transfers between devices: 53.3 us -> none  [on_device(): numer_all, denom_all = lax.psum((blurred, denom_cols), 'visit')]
    pallas_call x0 -> x1, Pallas kernels: none -> 52.8 us  [coadd(): pl.pallas_call(coadd_kernel, out_shape=jax.ShapeDtypeStruct((ROWS, EDGE),...]
    psum x1 -> x0, blocking collectives: 24.3 us -> none  [on_device(): numer_all, denom_all = lax.psum((blurred, denom_cols), 'visit')]
    ppermute x4 -> x0, starting transfers between devices: 17.8 us -> none  [the longest x2 12.1 us: extended(): lax.ppermute(lax.slice_in_dim(block, 0, width, axis=dim), axis, backward)]
    concatenate x4 -> x0, local copies, waits for them, and re-layouts: 6.83 us -> none  [the longest x1 5.41 us: extended(): block = jnp.concatenate([low, block, high], axis=dim)]
    unnamed x21 -> x1, local copies, waits for them, and re-layouts: 7.94 us -> 1.87 us
  transfers between devices with their start and end apart: 5 -> 0, of which waited for: 3 -> 0; matrix products, arithmetic and copies ran while one was open for 27% -> 0% of each run, Pallas kernels for 0% -> 0%
where the time goes in v2:
time: 54.8 us; the launch traced here: 54.7 us
  Pallas kernels  52.8 us (96%)
  local copies, waits for them, and re-layouts  1.87 us (3%)
    pallas_call x1, Pallas kernels, coadd(): pl.pallas_call(coadd_kernel, out_shape=jax.ShapeDtypeStruct((ROWS, EDGE),...  52.8 us
    unnamed x1, local copies, waits for them, and re-layouts  1.87 us

profile of v2, /device:TPU:24, one launch (start us, length us, event | category | flops | bytes accessed | tf_op | source)
XLA Modules:
  0.0 54.7 jit_solution(1448361311307888261)
XLA Ops:
  0.0 52.8 %coadd.1 = f32[1024,128]{1,0:T(8,128)} custom-call(s32[2,16]{1,0:T(2,128)} %bitcast.11, s32[1,64]{1,0:T(1,128)} %slot_hbm.1, s32[2,64]{1,0:T(2,128)} %bitcast.12, bf16[2,64]{1,0:T(2,128)(2,1)} %bitcast.13, bf16[1,64]{1,0:T(2,128)(2,1)} %inv_var_hbm.1, f32[25,1,25]{2,1,0:T(1,128)} %bitcast.10, bf16[64,128,128]{2,1,0:T(8,128)(2,1)} %bitcast.9), custom_call_target="tpu_custom_call" | custom-call | tf_op jit(solution)/shard_map/coadd/pallas_call | solution.py:606
  52.8 1.9 %copy.9 = f32[1024,128]{1,0:T(8,128)} copy(f32[1024,128]{1,0:T(8,128)} %coadd.1) | data formatting | bytes 1048576

commit v3 on v2

--- a/solution.py
+++ b/solution.py
@@ -29,7 +29,8 @@
 PACK = EDGE // SIDE
 HALVES = -(-2 * STEPS // PACK)
 DEPTH = STEPS * 2 * EDGE + HALVES * EDGE
-TILE_ROWS = PAIRS * SEGS
+HALF_PAIRS = PAIRS // 2
+HALF_ROWS = ROWS // 2
 F32 = jnp.float32
 BF16 = jnp.bfloat16
 
@@ -163,8 +164,6 @@
     own_part,
     pair_out,
     pair_in,
-    relay_out,
-    relay_in,
     chip_out,
     chip_in,
     local_sem,
@@ -176,8 +175,6 @@
     halo_recv,
     pair_send,
     pair_recv,
-    relay_send,
-    relay_recv,
     chip_send,
     chip_recv,
     weight_send,
@@ -369,7 +366,7 @@
     blank = jnp.zeros((EXT_PAIRS, SEGS, 2 * EDGE), BF16)
     centre[0] = blank
     centre[SLOT_COLS + 1] = blank
-    edges[EXT_PAIRS : EXT_PAIRS + 2] = jnp.zeros((2, SEGS, 2 * EDGE), F32)
+    edges[EXT_PAIRS : EXT_PAIRS + 2] = jnp.zeros((2, SEGS, 2 * EDGE), BF16)
 
     for side, (there, neighbour) in enumerate(sides_of):
 
@@ -445,12 +442,14 @@
 
     lane_seg = lax.broadcasted_iota(jnp.int32, (SEGS, EDGE), 1)
 
+    lane_pack = lane_seg.astype(BF16)
+
     def side_columns(w, carry):
         both = jnp.concatenate(
             [centre[w + k].reshape(EXT_PAIRS * SEGS, 2 * EDGE) for k in (0, 2)], axis=1
         )
         placed = jnp.dot(both, select[...], preferred_element_type=F32)
-        edges[0:EXT_PAIRS] = placed.reshape(EXT_PAIRS, SEGS, 2 * EDGE)
+        edges[0:EXT_PAIRS] = placed.astype(BF16).reshape(EXT_PAIRS, SEGS, 2 * EDGE)
 
         def pack(i, inner):
             for k in range(4):
@@ -459,8 +458,8 @@
                 for odd in range(2):
                     packed = rows[odd + PACK - 1]
                     for n in range(PACK - 2, -1, -1):
-                        packed = jnp.where(lane_seg < (n + 1) * SIDE, rows[odd + n], packed)
-                    sides[odd, w, g] = packed.astype(BF16)
+                        packed = jnp.where(lane_pack < (n + 1) * SIDE, rows[odd + n], packed)
+                    sides[odd, w, g] = packed
             return inner
 
         lax.fori_loop(0, EXT_PAIRS // 4, pack, 0)
@@ -471,84 +470,93 @@
     def pair_copy(k):
         return remote(pair_out.at[k], pair_in.at[k], pair_send.at[k], pair_recv.at[k], visit=partner)
 
-    ahead = 2 * lax.rem(chip + 1, chips) + core
-    behind = 2 * lax.rem(chip + chips - 1, chips) + core
-    ways = (ahead, behind)
-
-    def relay_copy(way):
+    ways = (
+        2 * lax.rem(chip + 1, chips) + core,
+        2 * lax.rem(chip + chips - 1, chips) + core,
+    )
+
+    def chip_copy(k, way):
         return remote(
-            relay_out.at[way], relay_in.at[way], relay_send.at[way], relay_recv.at[way], visit=ways[way]
-        )
-
-    def chip_copy(way):
-        return remote(
-            chip_out.at[way], chip_in.at[way], chip_send.at[way], chip_recv.at[way], visit=ways[way]
-        )
-
-    def total(k, half, r):
-        rows = pl.ds(pl.multiple_of(half * TILE_ROWS + r * EDGE, EDGE), EDGE)
-        return rows, own_part[rows, :] + pair_in[k, rows, :].astype(F32)
-
-    strips = TILE_ROWS // EDGE
+            chip_out.at[k, way],
+            chip_in.at[k, way],
+            chip_send.at[k, way],
+            chip_recv.at[k, way],
+            visit=ways[way],
+        )
+
+    def half_tile(w, half):
+        first = half * HALF_PAIRS
+        columns = [
+            centre[w + 1, pl.ds(first + t, HALF_PAIRS)].reshape(HALF_ROWS // 2, 2 * EDGE) for t in range(STEPS)
+        ]
+        for part in range(HALVES):
+            row = PACK * part
+            columns.append(
+                sides[row % 2, w, pl.ds(first + row // 2, HALF_PAIRS)].reshape(HALF_ROWS // 2, EDGE)
+            )
+        return columns
+
+    strip = 2 * EDGE
 
     def tile_step(i, carry):
         k = i // 2
         mine = lax.rem(i, 2)
-        distance = jnp.where(k == 0, 2, jnp.where(k == 1, 1, jnp.where(k == 2, chips - 1, 0)))
         to_core = jnp.where(mine == 1, core, 1 - core)
-        w = 2 * lax.rem(chip + distance, chips) + to_core
-        columns = [
-            centre[w + 1, t : t + PAIRS].reshape(TILE_ROWS, 2 * EDGE) for t in range(STEPS)
-        ]
-        for half in range(HALVES):
-            row = PACK * half
-            columns.append(sides[row % 2, w, row // 2 : row // 2 + PAIRS].reshape(TILE_ROWS, EDGE))
-        acc = jnp.dot(jnp.concatenate(columns, axis=1), taps[...], preferred_element_type=F32)
+        ahead = jnp.where(k == 0, 2, jnp.where(k == chips - 1, 0, 1))
+        behind = jnp.where(k == 0, 2, jnp.where(k == chips - 1, 0, chips - 1))
+        half = jnp.where(k == 1, 1, 0)
+        upper = half_tile(2 * lax.rem(chip + ahead, chips) + to_core, half)
+        lower = half_tile(2 * lax.rem(chip + behind, chips) + to_core, 1 - half)
+        both = jnp.concatenate(
+            [jnp.concatenate([a, b], axis=0) for a, b in zip(upper, lower)], axis=1
+        )
+        acc = jnp.dot(both, taps[...], preferred_element_type=F32)
+
+        def pieces():
+            for way in range(2):
+                for row_out in range(2):
+                    first = way * HALF_ROWS + row_out * (HALF_ROWS // 2)
+                    yield slice(first, first + HALF_ROWS // 2), acc[
+                        way * (HALF_ROWS // 2) : (way + 1) * (HALF_ROWS // 2),
+                        row_out * EDGE : (row_out + 1) * EDGE,
+                    ]
 
         @pl.when(mine == 0)
         def for_partner():
-            for row_out in range(2):
-                pair_out[k, row_out * TILE_ROWS : (row_out + 1) * TILE_ROWS, :] = acc[
-                    :, row_out * EDGE : (row_out + 1) * EDGE
-                ].astype(BF16)
+            for rows, value in pieces():
+                pair_out[k, rows, :] = value.astype(BF16)
             pair_copy(k).start()
 
         @pl.when(mine == 1)
         def for_this_core():
-            for row_out in range(2):
-                own_part[row_out * TILE_ROWS : (row_out + 1) * TILE_ROWS, :] = acc[
-                    :, row_out * EDGE : (row_out + 1) * EDGE
-                ]
+            for rows, value in pieces():
+                own_part[rows, :] = value
             pair_copy(k).wait_recv()
 
-            @pl.when(k == 0)
-            def opposite():
+            def send(extra):
                 for way in range(2):
+                    if extra:
+                        chip_copy(0, way).wait_recv()
 
                     def add(r, inner):
-                        _, value = total(k, way, r)
-                        relay_out[way, pl.ds(pl.multiple_of(r * EDGE, EDGE), EDGE), :] = value.astype(BF16)
+                        here = pl.ds(pl.multiple_of(r * strip, strip), strip)
+                        rows = pl.ds(pl.multiple_of(way * HALF_ROWS + r * strip, strip), strip)
+                        value = own_part[rows, :] + pair_in[k, rows, :].astype(F32)
+                        if extra:
+                            value = value + chip_in[0, way, here, :].astype(F32)
+                        chip_out[k, way, here, :] = value.astype(BF16)
                         return inner
 
-                    lax.fori_loop(0, strips, add, 0)
-                    relay_copy(way).start()
-
-            for way in range(2):
-
-                @pl.when(k == 1 + way)
-                def beside():
-                    relay_copy(way).wait_recv()
-                    for half in range(2):
-
-                        def add(r, inner):
-                            rows, value = total(k, half, r)
-                            if half == way:
-                                value = value + relay_in[way, pl.ds(pl.multiple_of(r * EDGE, EDGE), EDGE), :].astype(F32)
-                            chip_out[way, rows, :] = value.astype(BF16)
-                            return inner
-
-                        lax.fori_loop(0, strips, add, 0)
-                    chip_copy(way).start()
+                    lax.fori_loop(0, HALF_ROWS // strip, add, 0)
+                    chip_copy(k, way).start()
+
+            @pl.when(k < 2)
+            def plain():
+                send(False)
+
+            @pl.when(k == 2)
+            def relayed():
+                send(True)
 
         return carry
 
@@ -565,19 +573,24 @@
         jnp.where(lane_seg == wanted, jnp.broadcast_to(denom, (SEGS, EDGE)), 0.0), axis=1, keepdims=True
     )
     denom = jnp.broadcast_to(denom, (SEGS, EDGE))
-    for way in range(2):
-        chip_copy(way).wait_recv()
+    for k in (1, 2):
+        for way in range(2):
+            chip_copy(k, way).wait_recv()
 
     def finish(g, carry):
-        for row_out in range(2):
-            rows = pl.ds(pl.multiple_of(row_out * TILE_ROWS + g * SEGS, SEGS), SEGS)
-            value = own_part[rows, :] + pair_in[chips - 1, rows, :].astype(F32)
-            for way in range(2):
-                value = value + chip_in[way, rows, :].astype(F32)
-            out_ref[pl.ds(2 * g + row_out, SEGS, stride=SEG_ROWS), :] = value / denom
+        for half in range(2):
+            for row_out in range(2):
+                base = row_out * (HALF_ROWS // 2) + g * SEGS
+                here = pl.ds(pl.multiple_of(base, SEGS), SEGS)
+                rows = pl.ds(pl.multiple_of(half * HALF_ROWS + base, SEGS), SEGS)
+                value = own_part[rows, :] + pair_in[chips - 1, rows, :].astype(F32)
+                value = value + chip_in[1, 1 - half, here, :].astype(F32)
+                value = value + chip_in[2, half, here, :].astype(F32)
+                start = 2 * (half * HALF_PAIRS + g) + row_out
+                out_ref[pl.ds(start, SEGS, stride=SEG_ROWS), :] = value / denom
         return carry
 
-    lax.fori_loop(0, PAIRS, finish, 0)
+    lax.fori_loop(0, HALF_PAIRS, finish, 0)
 
     for side, (there, neighbour) in enumerate(sides_of):
 
@@ -591,9 +604,9 @@
 
     for k in range(chips):
         pair_copy(k).wait_send()
-    for way in range(2):
-        relay_copy(way).wait_send()
-        chip_copy(way).wait_send()
+    for k in range(chips - 1):
+        for way in range(2):
+            chip_copy(k, way).wait_send()
     for d in range(1, visits):
         weight_copy(d).wait_send()
 
@@ -637,17 +650,15 @@
             pltpu.VMEM((2, SLOT_COLS, HALO, EDGE), BF16),
             pltpu.VMEM((2, SLOT_COLS, HALO, EDGE), BF16),
             pltpu.VMEM((SLOT_COLS + 2, EXT_PAIRS, SEGS, 2 * EDGE), BF16),
-            pltpu.VMEM((EXT_PAIRS + 2, SEGS, 2 * EDGE), F32),
+            pltpu.VMEM((EXT_PAIRS + 2, SEGS, 2 * EDGE), BF16),
             pltpu.VMEM((2, SLOT_COLS, EXT_PAIRS, SEGS, EDGE), BF16),
             pltpu.VMEM((4 * EDGE, 2 * EDGE), BF16),
             pltpu.VMEM((DEPTH, 2 * EDGE), BF16),
             pltpu.VMEM((ROWS, EDGE), F32),
             pltpu.VMEM((chips, ROWS, EDGE), BF16),
             pltpu.VMEM((chips, ROWS, EDGE), BF16),
-            pltpu.VMEM((2, TILE_ROWS, EDGE), BF16),
-            pltpu.VMEM((2, TILE_ROWS, EDGE), BF16),
-            pltpu.VMEM((2, ROWS, EDGE), BF16),
-            pltpu.VMEM((2, ROWS, EDGE), BF16),
+            pltpu.VMEM((chips - 1, 2, HALF_ROWS, EDGE), BF16),
+            pltpu.VMEM((chips - 1, 2, HALF_ROWS, EDGE), BF16),
             dma((10,)),
             dma((2, CAP // CHUNK)),
             dma((2, CAP // CHUNK)),
@@ -657,10 +668,8 @@
             dma((2,)),
             dma((chips,)),
             dma((chips,)),
-            dma((2,)),
-            dma((2,)),
-            dma((2,)),
-            dma((2,)),
+            dma((chips - 1, 2)),
+            dma((chips - 1, 2)),
             dma((visits - 1,)),
             dma((visits - 1,)),
         ],

time: 54.8 us -> 49.7 us (0.907)
  Pallas kernels: 52.8 us -> 47.7 us
    pallas_call x1, Pallas kernels: 52.8 us -> 47.7 us  [coadd(): pl.pallas_call(coadd_kernel, out_shape=jax.ShapeDtypeStruct((ROWS, EDGE),...]
where the time goes in v3:
time: 49.7 us; the launch traced here: 49.6 us
  Pallas kernels  47.7 us (96%)
  local copies, waits for them, and re-layouts  1.87 us (4%)
    pallas_call x1, Pallas kernels, coadd(): pl.pallas_call(coadd_kernel, out_shape=jax.ShapeDtypeStruct((ROWS, EDGE),...  47.7 us
    unnamed x1, local copies, waits for them, and re-layouts  1.87 us

profile of v3, /device:TPU:24, one launch (start us, length us, event | category | flops | bytes accessed | tf_op | source)
XLA Modules:
  0.0 49.6 jit_solution(6103425095364987492)
XLA Ops:
  0.0 47.7 %coadd.1 = f32[1024,128]{1,0:T(8,128)} custom-call(s32[2,16]{1,0:T(2,128)} %bitcast.11, s32[1,64]{1,0:T(1,128)} %slot_hbm.1, s32[2,64]{1,0:T(2,128)} %bitcast.12, bf16[2,64]{1,0:T(2,128)(2,1)} %bitcast.13, bf16[1,64]{1,0:T(2,128)(2,1)} %inv_var_hbm.1, f32[25,1,25]{2,1,0:T(1,128)} %bitcast.10, bf16[64,128,128]{2,1,0:T(8,128)(2,1)} %bitcast.9), custom_call_target="tpu_custom_call" | custom-call | tf_op jit(solution)/shard_map/coadd/pallas_call | solution.py:619
  47.7 1.9 %copy.9 = f32[1024,128]{1,0:T(8,128)} copy(f32[1024,128]{1,0:T(8,128)} %coadd.1) | data formatting | bytes 1048576

commit v4 on v3

--- a/solution.py
+++ b/solution.py
@@ -31,6 +31,7 @@
 DEPTH = STEPS * 2 * EDGE + HALVES * EDGE
 HALF_PAIRS = PAIRS // 2
 HALF_ROWS = ROWS // 2
+LEAD = 3
 F32 = jnp.float32
 BF16 = jnp.bfloat16
 
@@ -99,12 +100,12 @@
 
 
 def build_select(select):
-    shape = (4 * EDGE, 2 * EDGE)
+    shape = (2 * EDGE, 2 * EDGE)
     source = lax.broadcasted_iota(jnp.int32, shape, 0)
     lane = lax.broadcasted_iota(jnp.int32, shape, 1)
     inner = lax.rem(lane, EDGE)
     q = lax.rem(inner, SIDE)
-    wanted = jnp.where(q < REACH, EDGE - REACH + q, 2 * EDGE + q - REACH) + (lane - inner)
+    wanted = jnp.where(q < REACH, EDGE - REACH + q, q - REACH) + (lane - inner)
     hit = (source == wanted) & (inner < PACK * SIDE)
     select[...] = jnp.where(hit, 1.0, 0.0).astype(BF16)
 
@@ -158,6 +159,7 @@
     halo_in,
     centre,
     edges,
+    fresh,
     sides,
     select,
     taps,
@@ -443,29 +445,43 @@
     lane_seg = lax.broadcasted_iota(jnp.int32, (SEGS, EDGE), 1)
 
     lane_pack = lane_seg.astype(BF16)
-
-    def side_columns(w, carry):
+    lane_all = lax.broadcasted_iota(jnp.int32, (EXT_PAIRS * SEGS, EDGE), 1).astype(BF16)
+    from_right = lane_all < EDGE // 2
+
+    def place_edges(w):
+        left, right = (centre[w + k].reshape(EXT_PAIRS * SEGS, 2 * EDGE) for k in (0, 2))
         both = jnp.concatenate(
-            [centre[w + k].reshape(EXT_PAIRS * SEGS, 2 * EDGE) for k in (0, 2)], axis=1
+            [
+                jnp.where(from_right, right[:, n * EDGE : (n + 1) * EDGE], left[:, n * EDGE : (n + 1) * EDGE])
+                for n in range(2)
+            ],
+            axis=1,
         )
         placed = jnp.dot(both, select[...], preferred_element_type=F32)
         edges[0:EXT_PAIRS] = placed.astype(BF16).reshape(EXT_PAIRS, SEGS, 2 * EDGE)
 
-        def pack(i, inner):
-            for k in range(4):
-                g = i * 4 + k
-                rows = [edges[g + n // 2, :, (n % 2) * EDGE : (n % 2 + 1) * EDGE] for n in range(PACK + 1)]
-                for odd in range(2):
-                    packed = rows[odd + PACK - 1]
-                    for n in range(PACK - 2, -1, -1):
-                        packed = jnp.where(lane_pack < (n + 1) * SIDE, rows[odd + n], packed)
-                    sides[odd, w, g] = packed
-            return inner
-
-        lax.fori_loop(0, EXT_PAIRS // 4, pack, 0)
+    def pack_edges():
+        for g in range(EXT_PAIRS):
+            rows = [edges[g + n // 2, :, (n % 2) * EDGE : (n % 2 + 1) * EDGE] for n in range(PACK + 1)]
+            for odd in range(2):
+                packed = rows[odd + PACK - 1]
+                for n in range(PACK - 2, -1, -1):
+                    packed = jnp.where(lane_pack < (n + 1) * SIDE, rows[odd + n], packed)
+                fresh[odd, g] = packed
+
+    def tile_at(turn):
+        distance = jnp.where(turn < 2, 2, jnp.where(turn < 6, 1 + 2 * lax.rem(turn, 2), 0))
+        is_mine = (turn == 1) | (turn == 4) | (turn == 5) | (turn == 7)
+        return 2 * lax.rem(chip + distance, chips) + jnp.where(is_mine, core, 1 - core)
+
+    def first_sides(turn, carry):
+        w = tile_at(turn)
+        place_edges(w)
+        pack_edges()
+        sides[:, w] = fresh[...]
         return carry
 
-    lax.fori_loop(0, SLOT_COLS, side_columns, 0)
+    lax.fori_loop(0, LEAD, first_sides, 0)
 
     def pair_copy(k):
         return remote(pair_out.at[k], pair_in.at[k], pair_send.at[k], pair_recv.at[k], visit=partner)
@@ -510,7 +526,10 @@
         both = jnp.concatenate(
             [jnp.concatenate([a, b], axis=0) for a, b in zip(upper, lower)], axis=1
         )
+        coming = tile_at(jnp.minimum(i + LEAD, SLOT_COLS - 1))
+        place_edges(coming)
         acc = jnp.dot(both, taps[...], preferred_element_type=F32)
+        pack_edges()
 
         def pieces():
             for way in range(2):
@@ -520,6 +539,8 @@
                         way * (HALF_ROWS // 2) : (way + 1) * (HALF_ROWS // 2),
                         row_out * EDGE : (row_out + 1) * EDGE,
                     ]
+
+        sides[:, coming] = fresh[...]
 
         @pl.when(mine == 0)
         def for_partner():
@@ -651,8 +672,9 @@
             pltpu.VMEM((2, SLOT_COLS, HALO, EDGE), BF16),
             pltpu.VMEM((SLOT_COLS + 2, EXT_PAIRS, SEGS, 2 * EDGE), BF16),
             pltpu.VMEM((EXT_PAIRS + 2, SEGS, 2 * EDGE), BF16),
+            pltpu.VMEM((2, EXT_PAIRS, SEGS, EDGE), BF16),
             pltpu.VMEM((2, SLOT_COLS, EXT_PAIRS, SEGS, EDGE), BF16),
-            pltpu.VMEM((4 * EDGE, 2 * EDGE), BF16),
+            pltpu.VMEM((2 * EDGE, 2 * EDGE), BF16),
             pltpu.VMEM((DEPTH, 2 * EDGE), BF16),
             pltpu.VMEM((ROWS, EDGE), F32),
             pltpu.VMEM((chips, ROWS, EDGE), BF16),

time: 49.7 us -> 47.5 us (0.956)
  Pallas kernels: 47.7 us -> 45.5 us
    pallas_call x1, Pallas kernels: 47.7 us -> 45.5 us  [coadd(): pl.pallas_call(coadd_kernel, out_shape=jax.ShapeDtypeStruct((ROWS, EDGE),...]
where the time goes in v4:
time: 47.5 us; the launch traced here: 47.3 us
  Pallas kernels  45.5 us (96%)
  local copies, waits for them, and re-layouts  1.87 us (4%)
    pallas_call x1, Pallas kernels, coadd(): pl.pallas_call(coadd_kernel, out_shape=jax.ShapeDtypeStruct((ROWS, EDGE),...  45.5 us
    unnamed x1, local copies, waits for them, and re-layouts  1.87 us

profile of v4, /device:TPU:24, one launch (start us, length us, event | category | flops | bytes accessed | tf_op | source)
XLA Modules:
  0.0 47.3 jit_solution(13001348573253874996)
XLA Ops:
  0.0 45.5 %coadd.1 = f32[1024,128]{1,0:T(8,128)} custom-call(s32[2,16]{1,0:T(2,128)} %bitcast.11, s32[1,64]{1,0:T(1,128)} %slot_hbm.1, s32[2,64]{1,0:T(2,128)} %bitcast.12, bf16[2,64]{1,0:T(2,128)(2,1)} %bitcast.13, bf16[1,64]{1,0:T(2,128)(2,1)} %inv_var_hbm.1, f32[25,1,25]{2,1,0:T(1,128)} %bitcast.10, bf16[64,128,128]{2,1,0:T(8,128)(2,1)} %bitcast.9), custom_call_target="tpu_custom_call" | custom-call | tf_op jit(solution)/shard_map/coadd/pallas_call | solution.py:640
  45.5 1.9 %copy.9 = f32[1024,128]{1,0:T(8,128)} copy(f32[1024,128]{1,0:T(8,128)} %coadd.1) | data formatting | bytes 1048576

commit v5 on v4

--- a/solution.py
+++ b/solution.py
@@ -430,7 +430,7 @@
                 centre[w + 1, g, :, row_in * EDGE : (row_in + 1) * EDGE] = rows.astype(BF16)
         return carry
 
-    lax.fori_loop(REACH // 2, REACH // 2 + PAIRS, to_pairs, 0)
+    lax.fori_loop(REACH // 2, REACH // 2 + PAIRS, to_pairs, 0, unroll=4)
     for side, (there, neighbour) in enumerate(sides_of):
 
         @pl.when(there)
@@ -439,8 +439,8 @@
 
     wide[:, 0:HALO, :] = halo_in[0].astype(F32)
     wide[:, HALO + ROWS : EXT_ROWS, :] = halo_in[1].astype(F32)
-    lax.fori_loop(0, REACH // 2, to_pairs, 0)
-    lax.fori_loop(REACH // 2 + PAIRS, EXT_PAIRS, to_pairs, 0)
+    lax.fori_loop(0, REACH // 2, to_pairs, 0, unroll=True)
+    lax.fori_loop(REACH // 2 + PAIRS, EXT_PAIRS, to_pairs, 0, unroll=True)
 
     lane_seg = lax.broadcasted_iota(jnp.int32, (SEGS, EDGE), 1)
 

time: 47.5 us -> 47 us (0.989)
  Pallas kernels: 45.5 us -> 44.9 us
    pallas_call x1, Pallas kernels: 45.5 us -> 44.9 us  [coadd(): pl.pallas_call(coadd_kernel, out_shape=jax.ShapeDtypeStruct((ROWS, EDGE),...]
where the time goes in v5:
time: 47 us; the launch traced here: 46.8 us
  Pallas kernels  44.9 us (96%)
  local copies, waits for them, and re-layouts  1.87 us (4%)
    pallas_call x1, Pallas kernels, coadd(): pl.pallas_call(coadd_kernel, out_shape=jax.ShapeDtypeStruct((ROWS, EDGE),...  44.9 us
    unnamed x1, local copies, waits for them, and re-layouts  1.87 us

profile of v5, /device:TPU:24, one launch (start us, length us, event | category | flops | bytes accessed | tf_op | source)
XLA Modules:
  0.0 46.8 jit_solution(4882858712111357469)
XLA Ops:
  0.0 44.9 %coadd.1 = f32[1024,128]{1,0:T(8,128)} custom-call(s32[2,16]{1,0:T(2,128)} %bitcast.11, s32[1,64]{1,0:T(1,128)} %slot_hbm.1, s32[2,64]{1,0:T(2,128)} %bitcast.12, bf16[2,64]{1,0:T(2,128)(2,1)} %bitcast.13, bf16[1,64]{1,0:T(2,128)(2,1)} %inv_var_hbm.1, f32[25,1,25]{2,1,0:T(1,128)} %bitcast.10, bf16[64,128,128]{2,1,0:T(8,128)(2,1)} %bitcast.9), custom_call_target="tpu_custom_call" | custom-call | tf_op jit(solution)/shard_map/coadd/pallas_call | solution.py:640
  45.0 1.9 %copy.9 = f32[1024,128]{1,0:T(8,128)} copy(f32[1024,128]{1,0:T(8,128)} %coadd.1) | data formatting | bytes 1048576
